TPU v7x, 128 devices: a whole 4x4x4 slice. The times are simulated.
128 devices in a mesh: ka: 64 (over z_lo, y, x, core), atoms: 2 (over z_hi).
Axes of the slice: x: 4, y: 4, z: 4 (z_hi: 2, z_lo: 2; z = z_hi * 2 + z_lo), core: 2. Of those that a mesh axis runs over, the one named last changes fastest.
Arguments:
- positions: float32 [64, 3, 65536], P('ka', None, 'atoms'), may hold values from 0 to 1
- counts: int32 [2, 3], P('atoms'), may hold values from 1 to 16384, 32768 in all within a row
- plan: int32 [8], replicated, may hold values from 0 to 63, as said below
- k_index: int32 [3, 8192], P(None, 'ka'), may hold values from -32 to 32, as said below
Outputs:
- factors: float32 [8, 6, 8192], P(None, None, 'ka')
Inputs may be any that keep to these rules, and one draw needn't show every extreme that they name: `plan`: the frame slots are distinct. `counts`: each row sums to 32768. `k_index`: the 8192 k-vectors (columns) are distinct and none is the zero vector.
All inputs are finite; a program needn't handle non-finite values.
Results may differ from a plain program's by a relative error of at most 0.0003.
Values sent between devices are 32-bit elements; how exact they have to be, the bound alone decides.
A program may use at most 192 MiB of HBM per device.

v0:
```python
import math

import jax
import jax.numpy as jnp
from jax import lax
from jax.sharding import PartitionSpec as P

FRAMES = 8


def spread(block, axis, owner):
    block = jnp.where(lax.axis_index(axis) == owner, block, jnp.zeros_like(block))
    return lax.psum(block, axis)


def frame_modes(coords, member, k_float):
    phase = k_float[0][:, None] * coords[0][None, :] + k_float[1][:, None] * coords[1][None, :]
    phase = (phase + k_float[2][:, None] * coords[2][None, :]) * (2.0 * math.pi)
    cosines = jnp.cos(phase)
    sines = jnp.sin(phase)
    dims = (((1,), (1,)), ((), ()))
    cos_part = lax.dot_general(
        member, cosines, dims, precision=lax.Precision.HIGHEST, preferred_element_type=jnp.float32
    )
    sin_part = lax.dot_general(
        member, sines, dims, precision=lax.Precision.HIGHEST, preferred_element_type=jnp.float32
    )
    return jnp.stack([cos_part, sin_part])


def transform(window_modes, total_atoms):
    frame_count = window_modes.shape[0]
    steps_index = jnp.arange(frame_count, dtype=jnp.float32)
    angles = steps_index[:, None] * steps_index[None, :] * (2.0 * math.pi / frame_count)
    cos_table = jnp.cos(angles)
    sin_table = jnp.sin(angles)
    cos_modes = window_modes[:, 0]
    sin_modes = window_modes[:, 1]
    high = lax.Precision.HIGHEST
    real_part = jnp.einsum("ft,tsk->fsk", cos_table, cos_modes, precision=high) + jnp.einsum(
        "ft,tsk->fsk", sin_table, sin_modes, precision=high
    )
    imag_part = jnp.einsum("ft,tsk->fsk", cos_table, sin_modes, precision=high) - jnp.einsum(
        "ft,tsk->fsk", sin_table, cos_modes, precision=high
    )
    first_species = jnp.array([0, 0, 0, 1, 1, 2], dtype=jnp.int32)
    second_species = jnp.array([0, 1, 2, 1, 2, 2], dtype=jnp.int32)
    product = (
        real_part[:, first_species] * real_part[:, second_species]
        + imag_part[:, first_species] * imag_part[:, second_species]
    )
    return product / (frame_count * total_atoms)


def species_rows(counts_row, atom_count):
    atom_index = jnp.arange(atom_count, dtype=jnp.int32)
    run_ends = jnp.cumsum(counts_row)
    run_starts = run_ends - counts_row
    return (
        (atom_index[None, :] >= run_starts[:, None]) & (atom_index[None, :] < run_ends[:, None])
    ).astype(jnp.float32)


def local(positions, counts, plan, k_index):
    atoms_here = positions.shape[2]
    total_atoms = atoms_here * lax.axis_size("atoms")
    member = species_rows(counts[0], atoms_here)
    k_float = k_index.astype(jnp.float32)
    frame_list = []
    for frame in range(FRAMES):
        coords = spread(positions[0], "ka", plan[frame])
        partial_modes = frame_modes(coords, member, k_float)
        partial_modes = lax.psum(partial_modes, "atoms")
        frame_list.append(partial_modes)
    window_modes = jnp.stack(frame_list)
    return transform(window_modes, total_atoms)


def solution(mesh):
    return jax.shard_map(
        local,
        mesh=mesh,
        in_specs=(P("ka", None, "atoms"), P("atoms", None), P(), P(None, "ka")),
        out_specs=P(None, None, "ka"),
        check_vma=False,
    )
```

profile of v0, /device:TPU:1, one launch (start us, length us, event | category | flops | bytes accessed | tf_op | source)
XLA Modules:
  0.0 1689.9 jit_solution(5395518006748752485)
XLA Ops:
  6.5 1.6 fusion.257
  13.2 3.9 broadcast_select_fusion
  17.1 1.6 copy_bitcast_fusion
  20.2 1.5 copy_bitcast_fusion.4
  21.8 1.6 copy_bitcast_fusion.6
  34.3 553.4 %all-reduce.4.cloned.1.call-done = (f32[3,32768]{1,0:T(4,128)}, f32[3,32768]{1,0:T(4,128)}, f32[3,32768]{1,0:T(4,128)}, f32[3,32768]{1,0:T(4,128)}, f32[3,32768]...) async-done(((f32[3,32768]{1,0:T(4,128)}, f32[3,32768]{1,0:T(4,128)}, f32[3,32768]{1,0:T(4,128)}, f32[3,32768]{1,0:T(4,128)}, ...) | async-done | bytes 3145744 | tf_op jit(solution)/shard_map/psum | solution.py:13
  587.7 1.8 fusion.249
  589.6 67.3 %fusion.186 = f32[1,3,128]{2,1,0:T(4,128)} fusion(f32[32768]{0:T(1024)S(1)} %bitcast.171, f32[32768]{0:T(1024)S(1)} %bitcast.173, f32[32768]{0:T(1024)S(1)} %bitcast.169, f32[128]{0:T(128)S(1)} %get-tuple-element.56, f32[128]{0:T(128)S(1)} %get-tuple-element.57, f32[128]{0:T(128)S(1)} %get-tuple-element.55, pred[3,32768]{1,0:T(4,128)(4,1)S(1)} %fusion.310), kind=kOutput, calls=%fused_computation.172 | convolution fusion | flops 176160768 | bytes 494592 | tf_op jit(solution)/shard_map/dot_general | solution.py:22
  656.8 68.1 %fusion.189 = f32[1,3,128]{2,1,0:T(4,128)} fusion(f32[32768]{0:T(1024)S(1)} %bitcast.172, f32[32768]{0:T(1024)S(1)} %bitcast.174, f32[32768]{0:T(1024)S(1)} %bitcast.170, f32[128]{0:T(128)S(1)} %get-tuple-element.56, f32[128]{0:T(128)S(1)} %get-tuple-element.57, f32[128]{0:T(128)S(1)} %get-tuple-element.55, pred[3,32768]{1,0:T(4,128)(4,1)S(1)} %fusion.312), kind=kOutput, calls=%fused_computation.173 | convolution fusion | flops 176160768 | bytes 494592 | tf_op jit(solution)/shard_map/dot_general | solution.py:25
  725.2 67.2 %fusion.180 = f32[1,3,128]{2,1,0:T(4,128)} fusion(f32[32768]{0:T(1024)S(1)} %bitcast.177, f32[32768]{0:T(1024)S(1)} %bitcast.179, f32[32768]{0:T(1024)S(1)} %bitcast.175, f32[128]{0:T(128)S(1)} %get-tuple-element.56, f32[128]{0:T(128)S(1)} %get-tuple-element.57, f32[128]{0:T(128)S(1)} %get-tuple-element.55, pred[3,32768]{1,0:T(4,128)(4,1)S(1)} %fusion.306), kind=kOutput, calls=%fused_computation.170 | convolution fusion | flops 176160768 | bytes 494592 | tf_op jit(solution)/shard_map/dot_general | solution.py:22
  792.4 67.8 %fusion.183 = f32[1,3,128]{2,1,0:T(4,128)} fusion(f32[32768]{0:T(1024)S(1)} %bitcast.178, f32[32768]{0:T(1024)S(1)} %bitcast.180, f32[32768]{0:T(1024)S(1)} %bitcast.176, f32[128]{0:T(128)S(1)} %get-tuple-element.56, f32[128]{0:T(128)S(1)} %get-tuple-element.57, f32[128]{0:T(128)S(1)} %get-tuple-element.55, pred[3,32768]{1,0:T(4,128)(4,1)S(1)} %fusion.308), kind=kOutput, calls=%fused_computation.171 | convolution fusion | flops 176160768 | bytes 494592 | tf_op jit(solution)/shard_map/dot_general | solution.py:25
  860.5 67.2 %fusion.174 = f32[1,3,128]{2,1,0:T(4,128)} fusion(f32[32768]{0:T(1024)S(1)} %bitcast.183, f32[32768]{0:T(1024)S(1)} %bitcast.185, f32[32768]{0:T(1024)S(1)} %bitcast.181, f32[128]{0:T(128)S(1)} %get-tuple-element.56, f32[128]{0:T(128)S(1)} %get-tuple-element.57, f32[128]{0:T(128)S(1)} %get-tuple-element.55, pred[3,32768]{1,0:T(4,128)(4,1)S(1)} %fusion.302), kind=kOutput, calls=%fused_computation.168 | convolution fusion | flops 176160768 | bytes 494592 | tf_op jit(solution)/shard_map/dot_general | solution.py:22
  927.7 68.1 %fusion.177 = f32[1,3,128]{2,1,0:T(4,128)} fusion(f32[32768]{0:T(1024)S(1)} %bitcast.184, f32[32768]{0:T(1024)S(1)} %bitcast.186, f32[32768]{0:T(1024)S(1)} %bitcast.182, f32[128]{0:T(128)S(1)} %get-tuple-element.56, f32[128]{0:T(128)S(1)} %get-tuple-element.57, f32[128]{0:T(128)S(1)} %get-tuple-element.55, pred[3,32768]{1,0:T(4,128)(4,1)S(1)} %fusion.304), kind=kOutput, calls=%fused_computation.169 | convolution fusion | flops 176160768 | bytes 494592 | tf_op jit(solution)/shard_map/dot_general | solution.py:25
  996.0 67.1 %fusion.168 = f32[1,3,128]{2,1,0:T(4,128)} fusion(f32[32768]{0:T(1024)S(1)} %bitcast.189, f32[32768]{0:T(1024)S(1)} %bitcast.191, f32[32768]{0:T(1024)S(1)} %bitcast.187, f32[128]{0:T(128)S(1)} %get-tuple-element.56, f32[128]{0:T(128)S(1)} %get-tuple-element.57, f32[128]{0:T(128)S(1)} %get-tuple-element.55, pred[3,32768]{1,0:T(4,128)(4,1)S(1)} %fusion.298), kind=kOutput, calls=%fused_computation.166 | convolution fusion | flops 176160768 | bytes 494592 | tf_op jit(solution)/shard_map/dot_general | solution.py:22
  1063.2 67.1 %fusion.171 = f32[1,3,128]{2,1,0:T(4,128)S(1)} fusion(f32[32768]{0:T(1024)S(1)} %bitcast.190, f32[32768]{0:T(1024)S(1)} %bitcast.192, f32[32768]{0:T(1024)S(1)} %bitcast.188, f32[128]{0:T(128)S(1)} %get-tuple-element.56, f32[128]{0:T(128)S(1)} %get-tuple-element.57, f32[128]{0:T(128)S(1)} %get-tuple-element.55, pred[3,32768]{1,0:T(4,128)(4,1)S(1)} %fusion.300), kind=kOutput, calls=%fused_computation.167 | convolution fusion | flops 176160768 | bytes 494592 | tf_op jit(solution)/shard_map/dot_general | solution.py:25
  1130.7 66.6 %fusion.162 = f32[1,3,128]{2,1,0:T(4,128)S(1)} fusion(f32[32768]{0:T(1024)S(1)} %bitcast.195, f32[32768]{0:T(1024)S(1)} %bitcast.197, f32[32768]{0:T(1024)S(1)} %bitcast.193, f32[128]{0:T(128)S(1)} %get-tuple-element.56, f32[128]{0:T(128)S(1)} %get-tuple-element.57, f32[128]{0:T(128)S(1)} %get-tuple-element.55, pred[3,32768]{1,0:T(4,128)(4,1)S(1)} %fusion.294), kind=kOutput, calls=%fused_computation.164 | convolution fusion | flops 176160768 | bytes 494592 | tf_op jit(solution)/shard_map/dot_general | solution.py:22
  1197.3 67.4 %fusion.165 = f32[1,3,128]{2,1,0:T(4,128)S(1)} fusion(f32[32768]{0:T(1024)S(1)} %bitcast.196, f32[32768]{0:T(1024)S(1)} %bitcast.198, f32[32768]{0:T(1024)S(1)} %bitcast.194, f32[128]{0:T(128)S(1)} %get-tuple-element.56, f32[128]{0:T(128)S(1)} %get-tuple-element.57, f32[128]{0:T(128)S(1)} %get-tuple-element.55, pred[3,32768]{1,0:T(4,128)(4,1)S(1)} %copy-done.13), kind=kOutput, calls=%fused_computation.165 | convolution fusion | flops 176160768 | bytes 494592 | tf_op jit(solution)/shard_map/dot_general | solution.py:25
  1265.7 66.5 %fusion.156 = f32[1,3,128]{2,1,0:T(4,128)S(1)} fusion(f32[32768]{0:T(1024)S(1)} %bitcast.201, f32[32768]{0:T(1024)S(1)} %bitcast.203, f32[32768]{0:T(1024)S(1)} %bitcast.199, f32[128]{0:T(128)S(1)} %get-tuple-element.56, f32[128]{0:T(128)S(1)} %get-tuple-element.57, f32[128]{0:T(128)S(1)} %get-tuple-element.55, pred[3,32768]{1,0:T(4,128)(4,1)S(1)} %copy-done.12), kind=kOutput, calls=%fused_computation.162 | convolution fusion | flops 176160768 | bytes 494592 | tf_op jit(solution)/shard_map/dot_general | solution.py:22
  1332.2 67.2 %fusion.159 = f32[1,3,128]{2,1,0:T(4,128)S(1)} fusion(f32[32768]{0:T(1024)S(1)} %bitcast.202, f32[32768]{0:T(1024)S(1)} %bitcast.204, f32[32768]{0:T(1024)S(1)} %bitcast.200, f32[128]{0:T(128)S(1)} %get-tuple-element.56, f32[128]{0:T(128)S(1)} %get-tuple-element.57, f32[128]{0:T(128)S(1)} %get-tuple-element.55, pred[3,32768]{1,0:T(4,128)(4,1)S(1)} %copy-done.11), kind=kOutput, calls=%fused_computation.163 | convolution fusion | flops 176160768 | bytes 494592 | tf_op jit(solution)/shard_map/dot_general | solution.py:25
  1400.4 66.6 %fusion.150 = f32[1,3,128]{2,1,0:T(4,128)S(1)} fusion(f32[32768]{0:T(1024)S(1)} %bitcast.207, f32[32768]{0:T(1024)S(1)} %bitcast.209, f32[32768]{0:T(1024)S(1)} %bitcast.205, f32[128]{0:T(128)S(1)} %get-tuple-element.56, f32[128]{0:T(128)S(1)} %get-tuple-element.57, f32[128]{0:T(128)S(1)} %get-tuple-element.55, pred[3,32768]{1,0:T(4,128)(4,1)S(1)} %copy-done.10), kind=kOutput, calls=%fused_computation.160 | convolution fusion | flops 176160768 | bytes 494592 | tf_op jit(solution)/shard_map/dot_general | solution.py:22
  1467.0 67.4 %fusion.153 = f32[1,3,128]{2,1,0:T(4,128)S(1)} fusion(f32[32768]{0:T(1024)S(1)} %bitcast.208, f32[32768]{0:T(1024)S(1)} %bitcast.210, f32[32768]{0:T(1024)S(1)} %bitcast.206, f32[128]{0:T(128)S(1)} %get-tuple-element.56, f32[128]{0:T(128)S(1)} %get-tuple-element.57, f32[128]{0:T(128)S(1)} %get-tuple-element.55, pred[3,32768]{1,0:T(4,128)(4,1)S(1)} %copy-done.9), kind=kOutput, calls=%fused_computation.161 | convolution fusion | flops 176160768 | bytes 494592 | tf_op jit(solution)/shard_map/dot_general | solution.py:25
  1535.4 66.5 %fusion.144 = f32[1,3,128]{2,1,0:T(4,128)S(1)} fusion(f32[32768]{0:T(1024)S(1)} %bitcast.165, f32[128]{0:T(128)S(1)} %get-tuple-element.56, f32[32768]{0:T(1024)S(1)} %bitcast.167, f32[128]{0:T(128)S(1)} %get-tuple-element.57, f32[32768]{0:T(1024)S(1)} %bitcast.163, f32[128]{0:T(128)S(1)} %get-tuple-element.55, pred[3,32768]{1,0:T(4,128)(4,1)S(1)} %copy-done.8), kind=kOutput, calls=%fused_computation.158 | convolution fusion | flops 176160768 | bytes 494592 | tf_op jit(solution)/shard_map/dot_general | solution.py:22
  1602.0 67.2 %fusion.147 = f32[1,3,128]{2,1,0:T(4,128)S(1)} fusion(f32[32768]{0:T(1024)S(1)} %bitcast.166, f32[128]{0:T(128)S(1)} %get-tuple-element.56, f32[32768]{0:T(1024)S(1)} %bitcast.168, f32[128]{0:T(128)S(1)} %get-tuple-element.57, f32[32768]{0:T(1024)S(1)} %bitcast.164, f32[128]{0:T(128)S(1)} %get-tuple-element.55, pred[3,32768]{1,0:T(4,128)(4,1)S(1)} %copy-done.7), kind=kOutput, calls=%fused_computation.159 | convolution fusion | flops 176160768 | bytes 494592 | tf_op jit(solution)/shard_map/dot_general | solution.py:25
  1669.3 9.2 all-reduce.1
  (107 shorter events, 20.8 us)
Async XLA Ops:
  6.5 581.2 %all-reduce.4.cloned.1.call-start = ((), (), s32[]{:S(2)}) async-start(), calls=%async_computation | async-start | bytes 8388608 | tf_op jit(solution)/shard_map/psum | solution.py:13
  26.7 7.0 copy-start.14
  26.7 7.0 copy-start.22
  26.7 7.0 copy-start.23
  656.8 68.1 %copy-start.6 = (f32[3,32768]{1,0:T(4,128)S(1)}, f32[3,32768]{1,0:T(4,128)}, u32[]{:S(2)}) copy-start(f32[3,32768]{1,0:T(4,128)} %get-tuple-element.11) | copy-start | bytes 1179652
  792.4 67.8 %copy-start.5 = (f32[3,32768]{1,0:T(4,128)S(1)}, f32[3,32768]{1,0:T(4,128)}, u32[]{:S(2)}) copy-start(f32[3,32768]{1,0:T(4,128)} %get-tuple-element.10) | copy-start | bytes 1179652
  927.7 68.1 %copy-start.4 = (f32[3,32768]{1,0:T(4,128)S(1)}, f32[3,32768]{1,0:T(4,128)}, u32[]{:S(2)}) copy-start(f32[3,32768]{1,0:T(4,128)} %get-tuple-element.9) | copy-start | bytes 1179652
  1063.2 67.1 %copy-start.3 = (f32[3,32768]{1,0:T(4,128)S(1)}, f32[3,32768]{1,0:T(4,128)}, u32[]{:S(2)}) copy-start(f32[3,32768]{1,0:T(4,128)} %get-tuple-element.8) | copy-start | bytes 1179652
  1130.7 66.6 %copy-start.13 = (pred[3,32768]{1,0:T(4,128)(4,1)S(1)}, pred[3,32768]{1,0:T(4,128)(4,1)}, u32[]{:S(2)}) copy-start(pred[3,32768]{1,0:T(4,128)(4,1)} %fusion.296) | copy-start | bytes 294916
  1197.3 67.5 %copy-start.2 = (f32[3,32768]{1,0:T(4,128)S(1)}, f32[3,32768]{1,0:T(4,128)}, u32[]{:S(2)}) copy-start(f32[3,32768]{1,0:T(4,128)} %get-tuple-element.7) | copy-start | bytes 1179652
  1264.7 1.0 copy-start.12
  1265.7 66.5 %copy-start.11 = (pred[3,32768]{1,0:T(4,128)(4,1)S(1)}, pred[3,32768]{1,0:T(4,128)(4,1)}, u32[]{:S(2)}) copy-start(pred[3,32768]{1,0:T(4,128)(4,1)} %fusion.292) | copy-start | bytes 294916
  1332.2 67.2 %copy-start.1 = (f32[3,32768]{1,0:T(4,128)S(1)}, f32[3,32768]{1,0:T(4,128)}, u32[]{:S(2)}) copy-start(f32[3,32768]{1,0:T(4,128)} %get-tuple-element.6) | copy-start | bytes 1179652
  1399.4 1.0 copy-start.10
  1400.4 66.6 %copy-start.9 = (pred[3,32768]{1,0:T(4,128)(4,1)S(1)}, pred[3,32768]{1,0:T(4,128)(4,1)}, u32[]{:S(2)}) copy-start(pred[3,32768]{1,0:T(4,128)(4,1)} %fusion.288) | copy-start | bytes 294916
  1466.9 67.5 %copy-start = (f32[3,32768]{1,0:T(4,128)S(1)}, f32[3,32768]{1,0:T(4,128)}, u32[]{:S(2)}) copy-start(f32[3,32768]{1,0:T(4,128)} %get-tuple-element.5) | copy-start | bytes 1179652
  1535.4 66.5 %copy-start.7 = (pred[3,32768]{1,0:T(4,128)(4,1)S(1)}, pred[3,32768]{1,0:T(4,128)(4,1)}, u32[]{:S(2)}) copy-start(pred[3,32768]{1,0:T(4,128)(4,1)} %fusion.284) | copy-start | bytes 294916
  1601.9 67.3 %copy-start.15 = (f32[1,3,128]{2,1,0:T(4,128)S(1)}, f32[1,3,128]{2,1,0:T(4,128)}, u32[]{:S(2)}) copy-start(f32[1,3,128]{2,1,0:T(4,128)} %fusion.186) | copy-start | bytes 4612
  1601.9 67.3 %copy-start.16 = (f32[1,3,128]{2,1,0:T(4,128)S(1)}, f32[1,3,128]{2,1,0:T(4,128)}, u32[]{:S(2)}) copy-start(f32[1,3,128]{2,1,0:T(4,128)} %fusion.189) | copy-start | bytes 4612
  1601.9 67.3 %copy-start.17 = (f32[1,3,128]{2,1,0:T(4,128)S(1)}, f32[1,3,128]{2,1,0:T(4,128)}, u32[]{:S(2)}) copy-start(f32[1,3,128]{2,1,0:T(4,128)} %fusion.180) | copy-start | bytes 4612
  1601.9 67.3 %copy-start.18 = (f32[1,3,128]{2,1,0:T(4,128)S(1)}, f32[1,3,128]{2,1,0:T(4,128)}, u32[]{:S(2)}) copy-start(f32[1,3,128]{2,1,0:T(4,128)} %fusion.183) | copy-start | bytes 4612
  1601.9 67.3 %copy-start.19 = (f32[1,3,128]{2,1,0:T(4,128)S(1)}, f32[1,3,128]{2,1,0:T(4,128)}, u32[]{:S(2)}) copy-start(f32[1,3,128]{2,1,0:T(4,128)} %fusion.174) | copy-start | bytes 4612
  1601.9 67.3 %copy-start.20 = (f32[1,3,128]{2,1,0:T(4,128)S(1)}, f32[1,3,128]{2,1,0:T(4,128)}, u32[]{:S(2)}) copy-start(f32[1,3,128]{2,1,0:T(4,128)} %fusion.177) | copy-start | bytes 4612
  1602.0 67.3 %copy-start.21 = (f32[1,3,128]{2,1,0:T(4,128)S(1)}, f32[1,3,128]{2,1,0:T(4,128)}, u32[]{:S(2)}) copy-start(f32[1,3,128]{2,1,0:T(4,128)} %fusion.168) | copy-start | bytes 4612
  (2 other events, 1.6 us)
Sparse Core Ops, SparseCore 0:
  23.5 564.2 all-reduce.3
where the time goes:
time: 1700 us; the launch traced here: 1690 us
  matrix products  1080 us (64%)
  waiting for transfers between devices  553 us (33%)
  between operations  19.1 us (1%)
  local copies, waits for them, and re-layouts  17.3 us (1%)
    psum x1, waiting for transfers between devices, spread(): return lax.psum(block, axis)  553 us
    dot_general x8, matrix products, frame_modes(): lax.dot_general(member, sines, dims, precision=lax.Precision.HIGHEST, pre...  540 us
    dot_general x8, matrix products, frame_modes(): lax.dot_general(member, cosines, dims, precision=lax.Precision.HIGHEST, p...  535 us
  transfers between devices with their start and end apart: 1, of which 1 were waited for; matrix products, arithmetic and copies ran while one was open for 1% of the time, Pallas kernels for 0%

commit v1 on v0

v1 whole, which is shorter than its diff:
```python
import jax, jax.numpy as jnp, numpy as np
from jax import lax
from jax.sharding import PartitionSpec as P
from jax.experimental import pallas as pl
from jax.experimental.pallas import tpu as pltpu

LINES = 88
COARSE = 13
CHUNK = 256
f32 = jnp.float32
bf16 = jnp.bfloat16

def fit_coefs():
    t = np.cos(np.pi * (np.arange(4000) + 0.5) / 4000) * 0.5
    u = t * t
    a = np.vander(u, 6, increasing=True)
    ps = np.linalg.lstsq(a * t[:, None], np.sin(np.pi * t), rcond=None)[0]
    pc = np.linalg.lstsq(a, np.cos(np.pi * t), rcond=None)[0]
    return [float(x) for x in ps], [float(x) for x in pc]

SIN_C, COS_C = fit_coefs()

def waves(cycles):
    t = cycles - jnp.round(cycles)
    u = t * t
    s = jnp.full_like(u, SIN_C[-1])
    for c in SIN_C[-2::-1]:
        s = s * u + c
    s = s * t
    q = jnp.full_like(u, COS_C[-1])
    for c in COS_C[-2::-1]:
        q = q * u + c
    twice = s + s
    return 1.0 - twice * s, twice * q

def split(x):
    hi = x.astype(bf16)
    lo = (x - hi.astype(f32)).astype(bf16)
    return hi, lo

def balanced(index, base, reach, mul, shift, below=0):
    upper = (((index + reach + base * below) * mul) >> shift) - below
    return upper, index - base * upper

def modes_kernel(counts, starts, pick_tile, pick_shift, x_ref, sign_ref, out_ref, e01, e2, fine, rhs, acc, grid):
    acc[...] = jnp.zeros_like(acc)
    ends = [counts[0]]
    for s in range(1, 3):
        ends.append(ends[-1] + counts[s])
    lane = lax.broadcasted_iota(jnp.int32, (1, CHUNK), 1)

    line = lax.broadcasted_iota(jnp.int32, (LINES, CHUNK), 0)
    q0, q1 = balanced(line, 13, 6, 79, 10)
    q0 = (5 * q0).astype(f32)
    q1 = (5 * q1).astype(f32)
    col = lax.broadcasted_iota(jnp.int32, (64, CHUNK), 0)
    r0, rest = balanced(col, 25, 12, 41, 10)
    r1, r2 = balanced(rest, 5, 2, 205, 10, 3)

    def chunk_step(i, _):
        off = pl.multiple_of(i * CHUNK, CHUNK)
        xs = [x_ref[d:d + 1, pl.ds(off, CHUNK)] for d in range(3)]
        xs = [x - jnp.round(x) for x in xs]
        c, s_ = waves(q0 * xs[0] + q1 * xs[1])
        e01[0:LINES] = c
        e01[LINES:2 * LINES] = s_
        depth = lax.broadcasted_iota(jnp.int32, (8, CHUNK), 0)
        c, s_ = waves((5 * depth).astype(f32) * xs[2])
        e2[0:8] = c
        e2[8:16] = s_
        c, s_ = waves(r0.astype(f32) * xs[0] + r1.astype(f32) * xs[1] + r2.astype(f32) * xs[2])
        fine[0:64] = c
        fine[64:128] = s_
        first = starts[i // (512 // CHUNK)] + lax.rem(i, 512 // CHUNK) * CHUNK

        def species_step(sp, _):
            end = jnp.where(sp == 0, ends[0], jnp.where(sp == 1, ends[1], ends[2]))
            begin = end - counts[sp]

            @pl.when(jnp.logical_and(begin < first + CHUNK, end > first))
            def _():
                where = lane + first
                mask = jnp.logical_and(where >= begin, where < end).astype(f32)
                hi, lo = split(fine[...] * mask)
                rhs[0:128, 0:CHUNK] = hi
                rhs[128:256, 0:CHUNK] = lo
                rhs[0:128, CHUNK:] = hi
                rhs[128:256, CHUNK:] = lo

                def depth_step(l, _):
                    row = jnp.where(l < 7, l, l + 2)
                    wave = e01[...] * e2[pl.ds(row, 1)]
                    hi, lo = split(wave)
                    lhs = jnp.concatenate([hi, lo], axis=1)
                    acc[sp, l] += lax.dot_general(lhs, rhs[...], (((1,), (1,)), ((), ())), preferred_element_type=f32)
                    return 0

                lax.fori_loop(0, COARSE, depth_step, 0, unroll=True)
            return 0
        lax.fori_loop(0, 3, species_step, 0)
        return 0

    lax.fori_loop(0, x_ref.shape[1] // CHUNK, chunk_step, 0)

    def halves(sp, l, part):
        rows = acc[sp, l, pl.ds(part * LINES, LINES), :]
        return rows[:, :128] + rows[:, 128:]

    def put(q2, sp, part, value):
        grid[pl.ds((q2 + 6) * LINES * 8 + part * 4 + sp, LINES, stride=8), :] = value

    for sp in range(3):
        put(0, sp, 0, halves(sp, 0, 0))
        put(0, sp, 1, halves(sp, 0, 1))
        for l in range(1, 7):
            cc, sc = halves(sp, l, 0), halves(sp, l, 1)
            cs, ss = halves(sp, l + 6, 0), halves(sp, l + 6, 1)
            put(l, sp, 0, cc - ss)
            put(-l, sp, 0, cc + ss)
            put(l, sp, 1, sc + cs)
            put(-l, sp, 1, sc - cs)

    lanes = lax.broadcasted_iota(jnp.int32, (8, 128), 1)

    def block_step(b, _):
        at_c = jnp.zeros((8, 128), f32)
        at_s = jnp.zeros((8, 128), f32)
        for j in range(128):
            row = pl.multiple_of(pick_tile[b, j], 8)
            tile = pltpu.roll(grid[pl.ds(row, 8), :], pick_shift[b, j], axis=1)
            at_c = jnp.where(lanes == j, tile, at_c)
            at_s = jnp.where(lanes == (j + 64) % 128, tile, at_s)
        at_s = pltpu.roll(at_s, 64, axis=1)
        sq = sign_ref[b, 0:1]
        sr = sign_ref[b, 1:2]
        real = at_c - sq * sr * pltpu.roll(at_s, 4, axis=0)
        imag = sq * at_c + sr * pltpu.roll(at_s, 4, axis=0)
        sub = lax.broadcasted_iota(jnp.int32, (8, 128), 0)
        out_ref[b] = jnp.where(sub < 4, real, imag)
        return 0

    lax.fori_loop(0, 64, block_step, 0)

def picks(k_index):
    n = k_index + 32
    q = ((n * 205) >> 10) - 6
    r = k_index - 5 * q
    jc = 13 * q[0] + q[1]
    sq = jnp.where(jc < 0, -1, 1)
    tile = (sq * q[2] + 6) * LINES + jnp.abs(jc)
    rc = 25 * r[0] + 5 * r[1] + r[2]
    sr = jnp.where(rc < 0, -1, 1)
    lane = jnp.arange(k_index.shape[1], dtype=jnp.int32) & 127
    shift = (lane - jnp.abs(rc)) & 127
    return tile * 8, shift, sq, sr

def call_modes(counts, starts, tiles, shifts, x, signs, interpret=False):
    smem = pl.BlockSpec(memory_space=pltpu.SMEM)
    vmem = pl.BlockSpec(memory_space=pltpu.VMEM)
    return pl.pallas_call(
        modes_kernel,
        out_shape=jax.ShapeDtypeStruct((64, 8, 128), f32),
        in_specs=[smem, smem, smem, smem, vmem, vmem],
        out_specs=vmem,
        scratch_shapes=[
            pltpu.VMEM((2 * LINES, CHUNK), f32),
            pltpu.VMEM((16, CHUNK), f32),
            pltpu.VMEM((128, CHUNK), f32),
            pltpu.VMEM((256, 2 * CHUNK), bf16),
            pltpu.VMEM((3, COARSE, 2 * LINES, 256), f32),
            pltpu.VMEM((13 * LINES * 8, 128), f32),
        ],
        compiler_params=pltpu.CompilerParams(vmem_limit_bytes=56 * 1024 * 1024),
        interpret=interpret,
    )(counts, starts, tiles, shifts, x, signs)


def transform(window, total_atoms):
    frames = window.shape[0]
    turn = np.arange(frames)[:, None] * np.arange(frames)[None, :] % frames
    cos_table = jnp.asarray(np.cos(2 * np.pi * turn / frames), f32)[:, :, None, None]
    sin_table = jnp.asarray(np.sin(2 * np.pi * turn / frames), f32)[:, :, None, None]
    c, s = window[None, :, 0:3], window[None, :, 4:7]
    real = jnp.sum(cos_table * c + sin_table * s, axis=1)
    imag = jnp.sum(cos_table * s - sin_table * c, axis=1)
    pairs = ((0, 0), (0, 1), (0, 2), (1, 1), (1, 2), (2, 2))
    out = [real[:, a] * real[:, b] + imag[:, a] * imag[:, b] for a, b in pairs]
    return jnp.stack(out, axis=1) / (frames * total_atoms)


def local(positions, counts, plan, k_index):
    atoms_here = positions.shape[2]
    devices = lax.axis_size("ka")
    piece = atoms_here // devices
    me = lax.axis_index("ka")
    pieces = jnp.transpose(positions[0].reshape(3, devices, piece), (1, 0, 2))
    slots = lax.all_to_all(pieces, "ka", 0, 0, tiled=True)
    window = slots[plan]
    groups = [[high * 16 + f * 2 + core for f in range(8)] for high in range(4) for core in range(2)]
    own = lax.all_to_all(window, "ka", 0, 0, axis_index_groups=groups, tiled=True)
    x = jnp.transpose(own, (1, 0, 2)).reshape(3, 8 * piece)
    starts = (me // 16 * 16 + jnp.arange(8, dtype=jnp.int32) * 2 + lax.rem(me, 2)) * piece
    tile, shift, sq, sr = picks(k_index)
    meta = lax.all_gather(jnp.stack([tile, shift, sq, sr]), "ka")
    modes = call_modes(counts[0], starts.astype(jnp.int32), meta[:, 0], meta[:, 1], x, meta[:, 2:].astype(f32))
    parts = lax.all_to_all(modes, "ka", 0, 0, tiled=True)
    total = jnp.sum(parts.reshape(4, 8, 2, 8, 128), axis=(0, 2))
    total = lax.psum(total, "atoms")
    return transform(total, atoms_here * lax.axis_size("atoms"))


def solution(mesh):
    return jax.shard_map(
        local,
        mesh=mesh,
        in_specs=(P("ka", None, "atoms"), P("atoms", None), P(), P(None, "ka")),
        out_specs=P(None, None, "ka"),
        check_vma=False,
    )
```

time: 1700 us -> 184 us (0.11)
  matrix products: 1080 us -> 0 us
  waiting for transfers between devices: 553 us -> 4.61 us
  blocking collectives: 9.23 us -> 108 us
  Pallas kernels: 0 us -> 47.8 us
  between operations: 19.1 us -> 0.17 us
    dot_general x20 -> x0, matrix products: 1080 us -> none  [the longest x8 540 us: frame_modes(): lax.dot_general(member, sines, dims, precision=lax.Precision.HIGHEST, pre...]
    psum x1 -> x0, waiting for transfers between devices: 553 us -> none  [spread(): return lax.psum(block, axis)]
    all_gather x0 -> x1, blocking collectives: none -> 82.8 us  [local(): meta = lax.all_gather(jnp.stack([tile, shift, sq, sr]), 'ka')]
    pallas_call x0 -> x1, Pallas kernels: none -> 47.8 us  [call_modes(): pl.pallas_call(modes_kernel, out_shape=jax.ShapeDtypeStruct((64, 8, 128),...]
  transfers between devices with their start and end apart: 1 -> 2, of which waited for: 1 -> 1; matrix products, arithmetic and copies ran while one was open for 1% -> 1% of each run, Pallas kernels for 0% -> 0%
where the time goes in v1:
time: 184 us; the launch traced here: 183 us
  blocking collectives  108 us (59%)
  Pallas kernels  47.8 us (26%)
  starting transfers between devices  13.8 us (8%)
  other arithmetic  4.88 us (3%)
  waiting for transfers between devices  4.61 us (3%)
  local copies, waits for them, and re-layouts  3.21 us (2%)
    all_gather x1, blocking collectives, local(): meta = lax.all_gather(jnp.stack([tile, shift, sq, sr]), 'ka')  82.8 us
    pallas_call x1, Pallas kernels, call_modes(): pl.pallas_call(modes_kernel, out_shape=jax.ShapeDtypeStruct((64, 8, 128),...  47.8 us
    all_to_all x1, blocking collectives, local(): parts = lax.all_to_all(modes, 'ka', 0, 0, tiled=True)  15.5 us
    all_to_all x1, starting transfers between devices, local(): slots = lax.all_to_all(pieces, 'ka', 0, 0, tiled=True)  10.5 us
    psum x1, blocking collectives, local(): total = lax.psum(total, 'atoms')  9.82 us
    all_to_all x1, waiting for transfers between devices, local(): lax.all_to_all(window, 'ka', 0, 0, axis_index_groups=groups, tiled=True)  4.61 us
  transfers between devices with their start and end apart: 2, of which 1 were waited for; matrix products, arithmetic and copies ran while one was open for 1% of the time, Pallas kernels for 0%

profile of v1, /device:TPU:1, one launch (start us, length us, event | category | flops | bytes accessed | tf_op | source)
XLA Modules:
  0.0 182.6 jit_solution(10476384837572928239)
XLA Ops:
  0.0 2.8 %reduce = f32[3,32768]{1,0:T(4,128)} reduce(f32[1,3,32768]{2,0,1:T(1,128)} %param.6, f32[]{:T(128)} %constant.73), dimensions={0}, to_apply=%param.6.reduce_sub_computation | reduce | bytes 786436 | tf_op args[0]
  2.8 0.0 copy-start.3
  2.8 10.5 %all-to-all-start = ((f32[64,3,512]{2,1,0:T(4,128)}), f32[64,3,512]{2,1,0:T(4,128)S(1)}, u32[]{:S(2)}, u32[]{:S(2)}) async-start(f32[64,3,512]{2,1,0:T(4,128)} %bitcast.4), calls=%async_computation | async-start | bytes 1048576 | tf_op jit(solution)/shard_map/all_to_all | solution.py:197
  13.3 0.0 copy-done.3
  13.4 82.8 %all-gather.1 = s32[64,4,128]{2,1,0:T(4,128)S(1)} all-gather(s32[1,4,128]{2,1,0:T(4,128)S(1)} %add_bitcast_fusion), channel_id=2, replica_groups=mesh['ka'=64,'atoms'=2] {'ka'}, dimensions={0}, use_global_device_ids=true | all-gather | bytes 133120 | tf_op jit(solution)/shard_map/all_gather | solution.py:204
  96.2 0.0 copy-start.4
  96.2 0.7 fusion
  96.9 0.0 copy-done.4
  96.9 0.7 slice_convert_fusion.sign_ref
  97.6 0.0 all-to-all-done
  97.6 1.2 gather_fusion
  98.8 3.3 %all-to-all-start.1 = ((f32[8,3,512]{2,1,0:T(4,128)}), f32[8,3,512]{2,1,0:T(4,128)S(1)}, u32[]{:S(2)}, u32[]{:S(2)}) async-start(f32[8,3,512]{2,1,0:T(4,128)} %gather_fusion), calls=%async_computation.1 | async-start | bytes 131072 | tf_op jit(solution)/shard_map/all_to_all | solution.py:200
  102.1 0.5 add_multiply_fusion.1.starts
  102.6 4.6 %all-to-all-done.1 = f32[8,3,512]{2,1,0:T(4,128)S(1)} async-done(((f32[8,3,512]{2,1,0:T(4,128)}), f32[8,3,512]{2,1,0:T(4,128)S(1)}, u32[]{:S(2)}, u32[]{:S(2)}) %all-to-all-start.1) | async-done | bytes 49184 | tf_op jit(solution)/shard_map/all_to_all | solution.py:200
  107.3 0.6 copy-done
  107.9 47.8 %shard_map.64 = f32[64,8,128]{2,1,0:T(8,128)} custom-call(s32[3]{0:T(128)} %bitcast.44, s32[8]{0:T(128)} %add_multiply_fusion.1.starts, s32[64,128]{1,0:T(8,128)} %bitcast.25, s32[64,128]{1,0:T(8,128)} %bitcast.24, f32[3,4096]{1,0:T(4,128)} %bitcast.23, f32[64,2,128]{2,1,0:T(2,128)} %slice_convert_fusion.sign_ref), custom_call_target="tpu_custom_call" | custom-call | tf_op jit(solution)/shard_map/pallas_call | solution.py:160
  155.7 15.5 %all_to_all.15 = f32[64,8,128]{2,1,0:T(8,128)S(1)} all-to-all(f32[64,8,128]{2,1,0:T(8,128)} %shard_map.64), channel_id=1, replica_groups=mesh['ka'=64,'atoms'=2] {'ka'}, dimensions={0} | all-to-all | bytes 524288 | tf_op jit(solution)/shard_map/all_to_all | solution.py:206
  171.2 9.8 %psum.7 = f32[8,8,128]{2,1,0:T(8,128)S(1)} all-reduce(f32[8,8,128]{2,1,0:T(8,128)S(1)} %reduce_sum.27), channel_id=1, replica_groups=mesh['ka'=64,'atoms'=2] {'atoms'}, use_global_device_ids=true, to_apply=%region_1.2 | all-reduce | flops 8192 | bytes 65536 | tf_op jit(solution)/shard_map/psum | solution.py:208
  181.1 0.0 copy-start.1
  181.1 0.0 copy-start.2
  181.1 0.7 copy-done.1
  181.7 0.0 copy-done.2
  181.8 0.1 add_reduce_fusion
  182.0 0.6 broadcast_multiply_fusion
  (19 shorter events, 0.1 us)
Async XLA Ops:
  2.8 10.5 %copy-start.3 = (s32[3,128]{1,0:T(4,128)S(1)}, s32[3,128]{1,0:T(4,128)}, u32[]{:S(2)}) copy-start(s32[3,128]{1,0:T(4,128)} %param.9) | copy-start | bytes 4612
  2.8 94.7 %all-to-all-start = ((f32[64,3,512]{2,1,0:T(4,128)}), f32[64,3,512]{2,1,0:T(4,128)S(1)}, u32[]{:S(2)}, u32[]{:S(2)}) async-start(f32[64,3,512]{2,1,0:T(4,128)} %bitcast.4), calls=%async_computation | async-start | bytes 1048576 | tf_op jit(solution)/shard_map/all_to_all | solution.py:197
  96.2 0.7 copy-start.4
  98.8 8.5 %all-to-all-start.1 = ((f32[8,3,512]{2,1,0:T(4,128)}), f32[8,3,512]{2,1,0:T(4,128)S(1)}, u32[]{:S(2)}, u32[]{:S(2)}) async-start(f32[8,3,512]{2,1,0:T(4,128)} %gather_fusion), calls=%async_computation.1 | async-start | bytes 131072 | tf_op jit(solution)/shard_map/all_to_all | solution.py:200
  107.3 0.6 copy-start
  181.1 0.7 copy-start.1
  181.1 0.7 copy-start.2

commit v2 on v1

v2 whole, which is shorter than its diff:
```python
import functools
import math

import jax
import jax.numpy as jnp
import numpy as np
from jax import lax
from jax.experimental import pallas as pl
from jax.experimental.pallas import tpu as pltpu
from jax.sharding import PartitionSpec as P

MESH = pl.DeviceIdType.MESH
FRAMES = 8
LINES = 88
COARSE = 13
CHUNK = 256
f32 = jnp.float32
bf16 = jnp.bfloat16

def fit_coefs():
    t = np.cos(np.pi * (np.arange(4000) + 0.5) / 4000) * 0.5
    u = t * t
    a = np.vander(u, 6, increasing=True)
    ps = np.linalg.lstsq(a * t[:, None], np.sin(np.pi * t), rcond=None)[0]
    pc = np.linalg.lstsq(a, np.cos(np.pi * t), rcond=None)[0]
    return [float(x) for x in ps], [float(x) for x in pc]

SIN_C, COS_C = fit_coefs()

def waves(cycles):
    t = cycles - jnp.round(cycles)
    u = t * t
    s = jnp.full_like(u, SIN_C[-1])
    for c in SIN_C[-2::-1]:
        s = s * u + c
    s = s * t
    q = jnp.full_like(u, COS_C[-1])
    for c in COS_C[-2::-1]:
        q = q * u + c
    twice = s + s
    return 1.0 - twice * s, twice * q

def split(x):
    hi = x.astype(bf16)
    lo = (x - hi.astype(f32)).astype(bf16)
    return hi, lo

def balanced(index, base, reach, mul, shift, below=0):
    upper = (((index + reach + base * below) * mul) >> shift) - below
    return upper, index - base * upper

def modes_kernel(counts, base, x_ref, word_ref, out_ref, e01, e2, fine, rhs, acc, grid, pick, pick_sem):
    piece = x_ref.shape[2] * 128
    per_piece = piece // CHUNK
    fetch = pltpu.make_async_copy(word_ref, pick, pick_sem)
    fetch.start()
    acc[...] = jnp.zeros_like(acc)
    ends = [counts[0, 0]]
    for s in range(1, 3):
        ends.append(ends[-1] + counts[0, s])
    lane = lax.broadcasted_iota(jnp.int32, (1, CHUNK), 1)

    line = lax.broadcasted_iota(jnp.int32, (LINES, CHUNK), 0)
    q0, q1 = balanced(line, 13, 6, 79, 10)
    q0 = (5 * q0).astype(f32)
    q1 = (5 * q1).astype(f32)
    col = lax.broadcasted_iota(jnp.int32, (64, CHUNK), 0)
    r0, rest = balanced(col, 25, 12, 41, 10)
    r1, r2 = balanced(rest, 5, 2, 205, 10, 3)

    def chunk_step(i, _):
        off = lax.rem(i, per_piece) * CHUNK
        xs = []
        for d in range(3):
            rows = [x_ref[i // per_piece, d, pl.ds(lax.rem(i, per_piece) * (CHUNK // 128) + n, 1)] for n in range(CHUNK // 128)]
            xs.append(jnp.concatenate(rows, axis=1))
        xs = [x - jnp.round(x) for x in xs]
        c, s_ = waves(q0 * xs[0] + q1 * xs[1])
        e01[0:LINES] = c
        e01[LINES:2 * LINES] = s_
        depth = lax.broadcasted_iota(jnp.int32, (8, CHUNK), 0)
        c, s_ = waves((5 * depth).astype(f32) * xs[2])
        e2[0:8] = c
        e2[8:16] = s_
        c, s_ = waves(r0.astype(f32) * xs[0] + r1.astype(f32) * xs[1] + r2.astype(f32) * xs[2])
        fine[0:64] = c
        fine[64:128] = s_
        first = (base[0] + 2 * (i // per_piece)) * piece + off

        def species_step(sp, _):
            end = jnp.where(sp == 0, ends[0], jnp.where(sp == 1, ends[1], ends[2]))
            begin = end - counts[0, sp]

            @pl.when(jnp.logical_and(begin < first + CHUNK, end > first))
            def _():
                where = lane + first
                mask = jnp.logical_and(where >= begin, where < end).astype(f32)
                hi, lo = split(fine[...] * mask)
                rhs[0:128, 0:CHUNK] = hi
                rhs[128:256, 0:CHUNK] = lo
                rhs[0:128, CHUNK:] = hi
                rhs[128:256, CHUNK:] = lo

                def depth_step(l, _):
                    row = jnp.where(l < 7, l, l + 2)
                    wave = e01[...] * e2[pl.ds(row, 1)]
                    hi, lo = split(wave)
                    lhs = jnp.concatenate([hi, lo], axis=1)
                    acc[sp, l] += lax.dot_general(lhs, rhs[...], (((1,), (1,)), ((), ())), preferred_element_type=f32)
                    return 0

                lax.fori_loop(0, COARSE, depth_step, 0, unroll=True)
            return 0
        lax.fori_loop(0, 3, species_step, 0)
        return 0

    lax.fori_loop(0, FRAMES * per_piece, chunk_step, 0)

    def halves(sp, l, part):
        rows = acc[sp, l, pl.ds(part * LINES, LINES), :]
        return rows[:, :128] + rows[:, 128:]

    def put(q2, sp, part, value):
        grid[pl.ds((q2 + 6) * LINES * 8 + part * 4 + sp, LINES, stride=8), :] = value

    for sp in range(3):
        put(0, sp, 0, halves(sp, 0, 0))
        put(0, sp, 1, halves(sp, 0, 1))
        for l in range(1, 7):
            cc, sc = halves(sp, l, 0), halves(sp, l, 1)
            cs, ss = halves(sp, l + 6, 0), halves(sp, l + 6, 1)
            put(l, sp, 0, cc - ss)
            put(-l, sp, 0, cc + ss)
            put(l, sp, 1, sc + cs)
            put(-l, sp, 1, sc - cs)

    lanes = lax.broadcasted_iota(jnp.int32, (8, 128), 1)

    fetch.wait()

    def block_step(b, _):
        at_c = jnp.zeros((8, 128), f32)
        at_s = jnp.zeros((8, 128), f32)
        for j in range(128):
            word = pick[b, 0, j]
            row = pl.multiple_of((word >> 9) * 8, 8)
            tile = pltpu.roll(grid[pl.ds(row, 8), :], word & 127, axis=1)
            at_c = jnp.where(lanes == j, tile, at_c)
            at_s = jnp.where(lanes == (j + 64) % 128, tile, at_s)
        at_s = pltpu.roll(at_s, 64, axis=1)
        word = word_ref[b]
        sq = jnp.where(((word >> 7) & 1) > 0, -1.0, 1.0)
        sr = jnp.where(((word >> 8) & 1) > 0, -1.0, 1.0)
        real = at_c - sq * sr * pltpu.roll(at_s, 4, axis=0)
        imag = sq * at_c + sr * pltpu.roll(at_s, 4, axis=0)
        sub = lax.broadcasted_iota(jnp.int32, (8, 128), 0)
        out_ref[b] = jnp.where(sub < 4, real, imag)
        return 0

    lax.fori_loop(0, 64, block_step, 0)

def picks(k_index):
    n = [k_index[d:d + 1] for d in range(3)]
    q, r = zip(*[balanced(v, 5, 2, 205, 10, 6) for v in n])
    jc = 13 * q[0] + q[1]
    sq = jnp.where(jc < 0, 1, 0)
    tile = (jnp.where(jc < 0, -q[2], q[2]) + 6) * LINES + jnp.abs(jc)
    rc = 25 * r[0] + 5 * r[1] + r[2]
    sr = jnp.where(rc < 0, 1, 0)
    lane = lax.broadcasted_iota(jnp.int32, rc.shape, 1)
    shift = (lane - jnp.abs(rc)) & 127
    return tile * 512 + sr * 256 + sq * 128 + shift


def call_modes(counts, base, x, words):
    smem = pl.BlockSpec(memory_space=pltpu.SMEM)
    vmem = pl.BlockSpec(memory_space=pltpu.VMEM)
    return pl.pallas_call(
        modes_kernel,
        out_shape=jax.ShapeDtypeStruct((64, 8, 128), f32),
        in_specs=[smem, smem, vmem, vmem],
        out_specs=vmem,
        scratch_shapes=[
            pltpu.VMEM((2 * LINES, CHUNK), f32),
            pltpu.VMEM((16, CHUNK), f32),
            pltpu.VMEM((128, CHUNK), f32),
            pltpu.VMEM((256, 2 * CHUNK), bf16),
            pltpu.VMEM((3, COARSE, 2 * LINES, 256), f32),
            pltpu.VMEM((13 * LINES * 8, 128), f32),
            pltpu.SMEM(words.shape, jnp.int32),
            pltpu.SemaphoreType.DMA,
        ],
        compiler_params=pltpu.CompilerParams(vmem_limit_bytes=20 * 1024 * 1024),
    )(counts, base, x, words)


def spread_kernel(plan, k_ref, pos_ref, x_ref, word_ref, slots, stage, word, send_sem, recv_sem, own_sem):
    me = lax.axis_index("ka")
    count = lax.axis_size("ka")
    rows = slots.shape[2]
    barrier = pltpu.get_barrier_semaphore()

    def greet(i, _):
        pl.semaphore_signal(barrier, inc=1, device_id={"ka": lax.rem(me + i, count)}, device_id_type=MESH)
        return 0

    lax.fori_loop(1, count, greet, 0)
    word[...] = picks(k_ref[...])
    pl.semaphore_wait(barrier, count - 1)

    def send(i, _):
        to = lax.rem(me + i, count)
        pltpu.make_async_remote_copy(
            src_ref=pos_ref.at[:, pl.ds(to * rows, rows)],
            dst_ref=slots.at[me],
            send_sem=send_sem.at[0],
            recv_sem=recv_sem.at[0],
            device_id={"ka": to},
            device_id_type=MESH,
        ).start()
        return 0

    lax.fori_loop(1, count, send, 0)
    keep = pltpu.make_async_copy(pos_ref.at[:, pl.ds(me * rows, rows)], slots.at[me], own_sem)
    keep.start()

    def send_word(i, _):
        pltpu.make_async_remote_copy(
            src_ref=word,
            dst_ref=word_ref.at[me],
            send_sem=send_sem.at[1],
            recv_sem=recv_sem.at[1],
            device_id={"ka": lax.rem(me + i, count)},
            device_id_type=MESH,
        ).start()
        return 0

    lax.fori_loop(1, count, send_word, 0)
    word_ref[me] = word[...]
    keep.wait()
    most = slots.at[pl.ds(0, count - 1)]
    pltpu.make_async_copy(most, most, recv_sem.at[0]).wait()
    frame = lax.rem(me // 2, FRAMES)
    base = me - 2 * frame
    for f in range(FRAMES):
        stage[f] = slots[plan[f]]

    def hand_on(i, _):
        to = lax.rem(frame + i, FRAMES)
        pltpu.make_async_remote_copy(
            src_ref=stage.at[to],
            dst_ref=x_ref.at[frame],
            send_sem=send_sem.at[2],
            recv_sem=recv_sem.at[2],
            device_id={"ka": base + 2 * to},
            device_id_type=MESH,
        ).start()
        return 0

    lax.fori_loop(1, FRAMES, hand_on, 0)
    x_ref[frame] = stage[frame]
    words = word_ref.at[pl.ds(0, count - 1)]
    pltpu.make_async_copy(words, words, recv_sem.at[1]).wait()
    rest = x_ref.at[pl.ds(0, FRAMES - 1)]
    pltpu.make_async_copy(rest, rest, recv_sem.at[2]).wait()
    pltpu.make_async_copy(most, most, send_sem.at[0]).wait()
    pltpu.make_async_copy(words, words, send_sem.at[1]).wait()
    pltpu.make_async_copy(rest, rest, send_sem.at[2]).wait()


def call_spread(plan, k_index, positions):
    smem = pl.BlockSpec(memory_space=pltpu.SMEM)
    vmem = pl.BlockSpec(memory_space=pltpu.VMEM)
    count = lax.axis_size("ka")
    rows = positions.shape[2] // (128 * count)
    positions = positions.reshape(3, rows * count, 128)
    return pl.pallas_call(
        spread_kernel,
        out_shape=(
            jax.ShapeDtypeStruct((FRAMES, 3, rows, 128), f32),
            jax.ShapeDtypeStruct((count, 1, k_index.shape[1]), jnp.int32),
        ),
        in_specs=[smem, vmem, pl.BlockSpec(memory_space=pl.ANY)],
        out_specs=(vmem, vmem),
        scratch_shapes=[
            pltpu.VMEM((count, 3, rows, 128), f32),
            pltpu.VMEM((FRAMES, 3, rows, 128), f32),
            pltpu.VMEM((1, k_index.shape[1]), jnp.int32),
            pltpu.SemaphoreType.DMA((3,)),
            pltpu.SemaphoreType.DMA((3,)),
            pltpu.SemaphoreType.DMA,
        ],
        compiler_params=pltpu.CompilerParams(collective_id=0, has_side_effects=True),
    )(plan, k_index, positions)


def factors_kernel(scale, modes_ref, out_ref, parts, send_sem, recv_sem, own_sem):
    me = lax.axis_index("ka")
    half = lax.axis_index("atoms")
    count = lax.axis_size("ka")
    barrier = pltpu.get_barrier_semaphore()

    def greet(i, _):
        for h in range(2):
            @pl.when(i + h > 0)
            def _():
                pl.semaphore_signal(
                    barrier, inc=1, device_id={"ka": lax.rem(me + i, count), "atoms": lax.rem(half + h, 2)},
                    device_id_type=MESH)
        return 0

    lax.fori_loop(0, count, greet, 0)
    pl.semaphore_wait(barrier, 2 * count - 1)
    slot = half * count + me

    def send(i, _):
        to = lax.rem(me + i, count)
        for h in range(2):
            @pl.when(i + h > 0)
            def _():
                pltpu.make_async_remote_copy(
                    src_ref=modes_ref.at[to],
                    dst_ref=parts.at[slot],
                    send_sem=send_sem,
                    recv_sem=recv_sem,
                    device_id={"ka": to, "atoms": lax.rem(half + h, 2)},
                    device_id_type=MESH,
                ).start()
        return 0

    lax.fori_loop(0, count, send, 0)
    keep = pltpu.make_async_copy(modes_ref.at[me], parts.at[slot], own_sem)
    keep.start()
    keep.wait()
    most = parts.at[pl.ds(0, 2 * count - 1)]
    pltpu.make_async_copy(most, most, recv_sem).wait()
    window = []
    for f in range(FRAMES):
        total = None
        for high in range(2 * count // 16):
            for core in range(2):
                part = parts[high * 16 + f * 2 + core]
                total = part if total is None else total + part
        window.append(total)
    upper = lax.broadcasted_iota(jnp.int32, (8, 128), 0) < 4
    crossed = [jnp.where(upper, 1.0, -1.0) * pltpu.roll(w, 4, axis=0) for w in window]
    pairs = ((0, 0), (0, 1), (0, 2), (1, 1), (1, 2), (2, 2))
    for f in range(FRAMES):
        wave = window[0]
        for t in range(1, FRAMES):
            turn = 2 * math.pi * (f * t % FRAMES) / FRAMES
            wave = wave + math.cos(turn) * window[t] + math.sin(turn) * crossed[t]
        for p, (a, b) in enumerate(pairs):
            value = wave[a:a + 1] * wave[b:b + 1] + wave[4 + a:5 + a] * wave[4 + b:5 + b]
            out_ref[f, p:p + 1] = value * scale
    pltpu.make_async_copy(most, most, send_sem).wait()


def call_factors(modes, total_atoms):
    vmem = pl.BlockSpec(memory_space=pltpu.VMEM)
    count = lax.axis_size("ka")
    return pl.pallas_call(
        functools.partial(factors_kernel, 1.0 / (FRAMES * total_atoms)),
        out_shape=jax.ShapeDtypeStruct((FRAMES, 6, modes.shape[2]), f32),
        in_specs=[vmem],
        out_specs=vmem,
        scratch_shapes=[
            pltpu.VMEM((2 * count, 8, modes.shape[2]), f32),
            pltpu.SemaphoreType.DMA,
            pltpu.SemaphoreType.DMA,
            pltpu.SemaphoreType.DMA,
        ],
        compiler_params=pltpu.CompilerParams(collective_id=1, has_side_effects=True),
    )(modes)


def local(positions, counts, plan, k_index):
    me = lax.axis_index("ka")
    x, words = call_spread(plan, k_index, positions)
    first = me - lax.rem(me // 2, FRAMES) * 2
    modes = call_modes(counts, first.astype(jnp.int32).reshape(1), x, words)
    return call_factors(modes, positions.shape[2] * lax.axis_size("atoms"))


def solution(mesh):
    return jax.shard_map(
        local,
        mesh=mesh,
        in_specs=(P("ka", None, "atoms"), P("atoms", None), P(), P(None, "ka")),
        out_specs=P(None, None, "ka"),
        check_vma=False,
    )
```

time: 184 us -> 92.3 us (0.50)
  blocking collectives: 108 us -> 0 us
  Pallas kernels: 47.8 us -> 87.6 us
  starting transfers between devices: 13.8 us -> 0 us
  other arithmetic: 4.88 us -> 0 us
  waiting for transfers between devices: 4.61 us -> 0 us
    all_gather x1 -> x0, blocking collectives: 82.8 us -> none  [local(): meta = lax.all_gather(jnp.stack([tile, shift, sq, sr]), 'ka')]
    pallas_call x0 -> x2, Pallas kernels: none -> 40 us  [the longest x1 20.6 us: call_spread(): pl.pallas_call(spread_kernel, out_shape=(jax.ShapeDtypeStruct((FRAMES, 3,...]
    all_to_all x1 -> x0, blocking collectives: 15.5 us -> none  [local(): parts = lax.all_to_all(modes, 'ka', 0, 0, tiled=True)]
    all_to_all x2 -> x0, starting transfers between devices: 13.8 us -> none  [the longest x1 10.5 us: local(): slots = lax.all_to_all(pieces, 'ka', 0, 0, tiled=True)]
    psum x1 -> x0, blocking collectives: 9.82 us -> none  [local(): total = lax.psum(total, 'atoms')]
    all_to_all x2 -> x0, waiting for transfers between devices: 4.61 us -> none  [the longest x1 4.61 us: local(): lax.all_to_all(window, 'ka', 0, 0, axis_index_groups=groups, tiled=True)]
    unnamed x7 -> x0, other arithmetic: 2.88 us -> none
  transfers between devices with their start and end apart: 2 -> 0, of which waited for: 1 -> 0; matrix products, arithmetic and copies ran while one was open for 1% -> 0% of each run, Pallas kernels for 0% -> 0%
where the time goes in v2:
time: 92.3 us; the launch traced here: 91.9 us
  Pallas kernels  87.6 us (95%)
  local copies, waits for them, and re-layouts  4.26 us (5%)
    pallas_call x1, Pallas kernels, call_modes(): pl.pallas_call(modes_kernel, out_shape=jax.ShapeDtypeStruct((64, 8, 128),...  47.6 us
    pallas_call x1, Pallas kernels, call_spread(): pl.pallas_call(spread_kernel, out_shape=(jax.ShapeDtypeStruct((FRAMES, 3,...  20.6 us
    pallas_call x1, Pallas kernels, call_factors(): pl.pallas_call(functools.partial(factors_kernel, 1.0 / (FRAMES * total_at...  19.4 us
    unnamed x8, local copies, waits for them, and re-layouts  2.89 us

profile of v2, /device:TPU:1, one launch (start us, length us, event | category | flops | bytes accessed | tf_op | source)
XLA Modules:
  0.0 91.9 jit_solution(9903656049591541641)
XLA Ops:
  0.0 20.6 %shard_map.46 = (f32[8,3,4,128]{3,2,1,0:T(4,128)}, s32[64,1,128]{2,1,0:T(1,128)}) custom-call(s32[8]{0:T(128)} %plan.1, s32[3,128]{1,0:T(4,128)} %k_ref.1, f32[3,256,128]{2,1,0:T(8,128)} %bitcast.2), custom_call_target="tpu_custom_call" | custom-call | tf_op jit(solution)/shard_map/pallas_call | solution.py:277
  20.6 0.0 copy-start.3
  20.6 0.6 copy-done.3
  21.3 0.0 copy-start.1
  21.3 0.8 copy-done.1
  22.1 0.0 copy-start.2
  22.1 0.8 copy-done.2
  22.8 47.6 %shard_map.47.modes_ref = f32[64,8,128]{2,1,0:T(8,128)S(1)} custom-call(s32[1,3]{1,0:T(1,128)S(1)} %copy-done.3, s32[1]{0:T(128)} %bitcast.base, f32[8,3,4,128]{3,2,1,0:T(4,128)S(1)} %copy-done.1, s32[64,1,128]{2,1,0:T(1,128)S(1)} %copy-done.2), custom_call_target="tpu_custom_call" | custom-call | tf_op jit(solution)/shard_map/pallas_call | solution.py:178
  70.4 0.0 copy-start
  70.4 0.7 copy-done
  71.1 19.4 %shard_map.48 = f32[8,6,128]{2,1,0:T(8,128)} custom-call(f32[64,8,128]{2,1,0:T(8,128)} %copy-done), custom_call_target="tpu_custom_call" | custom-call | tf_op jit(solution)/shard_map/pallas_call | solution.py:362
  90.6 1.4 %copy.5 = f32[8,6,128]{2,0,1:T(8,128)} copy(f32[8,6,128]{2,1,0:T(8,128)} %shard_map.48) | data formatting | bytes 49152 | tf_op jit(solution)/shard_map/pallas_call | solution.py:362
Async XLA Ops:
  20.6 0.7 copy-start.3
  21.3 0.8 copy-start.1
  22.1 0.8 copy-start.2
  70.4 0.7 copy-start

commit v3 on v2

v3 whole, which is shorter than its diff:
```python
import functools
import math

import jax
import jax.numpy as jnp
import numpy as np
from jax import lax
from jax.experimental import pallas as pl
from jax.experimental.pallas import tpu as pltpu
from jax.sharding import PartitionSpec as P

MESH = pl.DeviceIdType.MESH
FRAMES = 8
LINES = 88
COARSE = 13
CHUNK = 256
GROUP = 4
f32 = jnp.float32
bf16 = jnp.bfloat16

def fit_coefs():
    t = np.cos(np.pi * (np.arange(4000) + 0.5) / 4000) * 0.5
    u = t * t
    a = np.vander(u, 5, increasing=True)
    ps = np.linalg.lstsq(a * t[:, None], np.sin(np.pi * t), rcond=None)[0]
    pc = np.linalg.lstsq(a, np.cos(np.pi * t), rcond=None)[0]
    return [float(x) for x in ps], [float(x) for x in pc]

SIN_C, COS_C = fit_coefs()

def waves(cycles):
    t = cycles - jnp.round(cycles)
    u = t * t
    s = jnp.full_like(u, SIN_C[-1])
    for c in SIN_C[-2::-1]:
        s = s * u + c
    s = s * t
    q = jnp.full_like(u, COS_C[-1])
    for c in COS_C[-2::-1]:
        q = q * u + c
    twice = s + s
    return 1.0 - twice * s, twice * q

def split(x):
    hi = x.astype(bf16)
    lo = (x - hi.astype(f32)).astype(bf16)
    return hi, lo

def balanced(index, base, reach, mul, shift, below=0):
    upper = (((index + reach + base * below) * mul) >> shift) - below
    return upper, index - base * upper

def lattice_kernel(counts, base, x_ref, grid, e01_a, e01_b, e2_a, e2_b, rhs_a, rhs_b, acc):
    acc[...] = jnp.zeros_like(acc)
    pieces, _, rows, _ = x_ref.shape
    piece = rows * 128
    per_piece = piece // CHUNK
    chunks = pieces * per_piece
    end = [counts[0, 0], counts[0, 0] + counts[0, 1]]
    below = []
    for e in end:
        total = 0
        for p in range(pieces):
            total = total + jnp.clip(e - (base[0] + 2 * p) * piece, 0, piece)
        below.append(total)
    cut0, cut1 = below
    turn0 = (cut0 + CHUNK - 1) // CHUNK
    turn1 = turn0 + (cut1 + CHUNK - 1) // CHUNK - cut0 // CHUNK

    lane = lax.broadcasted_iota(jnp.int32, (1, CHUNK), 1)
    line = lax.broadcasted_iota(jnp.int32, (LINES, CHUNK), 0)
    q0, q1 = [(5 * q).astype(f32) for q in balanced(line, 13, 6, 79, 10)]
    q2 = (5 * lax.broadcasted_iota(jnp.int32, (8, CHUNK), 0)).astype(f32)
    r0, rest = balanced(lax.broadcasted_iota(jnp.int32, (64, CHUNK), 0), 25, 12, 41, 10)
    r1, r2 = balanced(rest, 5, 2, 205, 10, 3)
    r0, r1, r2 = r0.astype(f32), r1.astype(f32), r2.astype(f32)

    def visit(v):
        kind = (v >= turn0).astype(jnp.int32) + (v >= turn1).astype(jnp.int32)
        chunk = jnp.where(kind == 0, v, jnp.where(kind == 1, v - turn0 + cut0 // CHUNK, v - turn1 + cut1 // CHUNK))
        first = jnp.where(kind == 0, 0, jnp.where(kind == 1, cut0, cut1))
        last = jnp.where(kind == 0, cut0, jnp.where(kind == 1, cut1, chunks * CHUNK))
        return kind, chunk, first, last

    def prepare(v, e01, e2, rhs):
        _, chunk, first, last = visit(v)
        here = jnp.minimum(chunk, chunks - 1)
        xs = []
        for d in range(3):
            at = lax.rem(here, per_piece) * (CHUNK // 128)
            parts = [x_ref[here // per_piece, d, pl.ds(at + n, 1)] for n in range(CHUNK // 128)]
            whole = jnp.concatenate(parts, axis=1)
            xs.append(whole - jnp.round(whole))
        c, s = waves(q0 * xs[0] + q1 * xs[1])
        e01[0:LINES] = c
        e01[LINES:] = s
        c, s = waves(q2 * xs[2])
        e2[0:8] = c
        e2[8:16] = s
        where = chunk * CHUNK + lane
        mask = jnp.logical_and(where >= first, where < last).astype(f32)
        c, s = waves(r0 * xs[0] + r1 * xs[1] + r2 * xs[2])
        hi, lo = split(jnp.concatenate([c * mask, s * mask], axis=0))
        rhs[0:128] = hi
        rhs[128:256] = lo

    def gather(v, e01, e2, rhs):
        kind = visit(v)[0]
        weights = rhs[...]
        for l in range(COARSE):
            row = l if l < 7 else l + 2
            hi, lo = split(e01[...] * e2[row:row + 1])
            lhs = jnp.concatenate([hi, lo], axis=0)
            p = lax.dot_general(lhs, weights, (((1,), (1,)), ((), ())), preferred_element_type=f32)
            p = p[0:2 * LINES] + p[2 * LINES:]
            acc[kind, l] += p[:, :128] + p[:, 128:]

    buffers = ((e01_a, e2_a, rhs_a), (e01_b, e2_b, rhs_b))
    prepare(0, *buffers[0])

    def pair(i, _):
        prepare(2 * i + 1, *buffers[1])
        gather(2 * i, *buffers[0])
        prepare(2 * i + 2, *buffers[0])
        gather(2 * i + 1, *buffers[1])
        return 0

    lax.fori_loop(0, (chunks + 2) // 2, pair, 0)

    front = lax.broadcasted_iota(jnp.int32, (LINES, 128), 1) < 64

    def put(q2, sp, a, b):
        plus = b + pltpu.roll(a, 64, axis=1)
        minus = a - pltpu.roll(b, 64, axis=1)
        at = (q2 + 6) * LINES * 8 + sp
        grid[pl.ds(at, LINES, stride=8), :] = jnp.where(front, minus, plus)
        grid[pl.ds(at + 4, LINES, stride=8), :] = jnp.where(front, plus, -minus)

    for sp in range(3):
        put(0, sp, acc[sp, 0, 0:LINES], acc[sp, 0, LINES:])
        for l in range(1, 7):
            cc, sc = acc[sp, l, 0:LINES], acc[sp, l, LINES:]
            cs, ss = acc[sp, l + 6, 0:LINES], acc[sp, l + 6, LINES:]
            put(l, sp, cc - ss, sc + cs)
            put(-l, sp, cc + ss, sc - cs)


def call_lattice(counts, base, x):
    smem = pl.BlockSpec(memory_space=pltpu.SMEM)
    vmem = pl.BlockSpec(memory_space=pltpu.VMEM)
    return pl.pallas_call(
        lattice_kernel,
        out_shape=jax.ShapeDtypeStruct((13 * LINES * 8, 128), f32),
        in_specs=[smem, smem, vmem],
        out_specs=vmem,
        scratch_shapes=[pltpu.VMEM((2 * LINES, CHUNK), f32)] * 2
        + [pltpu.VMEM((16, CHUNK), f32)] * 2
        + [pltpu.VMEM((256, CHUNK), bf16)] * 2
        + [pltpu.VMEM((3, COARSE, 2 * LINES, 128), f32)],
        compiler_params=pltpu.CompilerParams(vmem_limit_bytes=24 * 1024 * 1024),
    )(counts, base, x)


def picks(k_index):
    n = [k_index[d:d + 1] for d in range(3)]
    q, r = zip(*[balanced(v, 5, 2, 205, 10, 6) for v in n])
    jc = 13 * q[0] + q[1]
    sq = jnp.where(jc < 0, 1, 0)
    tile = (jnp.where(jc < 0, -q[2], q[2]) + 6) * LINES + jnp.abs(jc)
    rc = 25 * r[0] + 5 * r[1] + r[2]
    sr = jnp.where(rc < 0, 1, 0)
    lane = lax.broadcasted_iota(jnp.int32, rc.shape, 1)
    shift = (lane - jnp.abs(rc) - 64 * (sr ^ sq)) & 127
    return tile * 256 + sq * 128 + shift


def spread_kernel(plan, k_ref, pos_ref, x_ref, word_ref, slots, stage, word, send_sem, recv_sem, own_sem):
    me = lax.axis_index("ka")
    count = lax.axis_size("ka")
    rows = slots.shape[2]
    barrier = pltpu.get_barrier_semaphore()

    def greet(i, _):
        pl.semaphore_signal(barrier, inc=1, device_id={"ka": lax.rem(me + i, count)}, device_id_type=MESH)
        return 0

    lax.fori_loop(1, count, greet, 0)
    word[...] = picks(k_ref[...])
    pl.semaphore_wait(barrier, count - 1)

    def send(i, _):
        to = lax.rem(me + i, count)
        pltpu.make_async_remote_copy(
            src_ref=pos_ref.at[:, pl.ds(to * rows, rows)],
            dst_ref=slots.at[me],
            send_sem=send_sem.at[0],
            recv_sem=recv_sem.at[0],
            device_id={"ka": to},
            device_id_type=MESH,
        ).start()
        return 0

    lax.fori_loop(1, count, send, 0)
    keep = pltpu.make_async_copy(pos_ref.at[:, pl.ds(me * rows, rows)], slots.at[me], own_sem)
    keep.start()

    def send_word(i, _):
        pltpu.make_async_remote_copy(
            src_ref=word,
            dst_ref=word_ref.at[me],
            send_sem=send_sem.at[1],
            recv_sem=recv_sem.at[1],
            device_id={"ka": lax.rem(me + i, count)},
            device_id_type=MESH,
        ).start()
        return 0

    lax.fori_loop(1, count, send_word, 0)
    word_ref[me] = word[...]
    keep.wait()
    most = slots.at[pl.ds(0, count - 1)]
    pltpu.make_async_copy(most, most, recv_sem.at[0]).wait()
    frame = lax.rem(me // 2, FRAMES)
    base = me - 2 * frame
    for f in range(FRAMES):
        stage[f] = slots[plan[f]]

    def hand_on(i, _):
        to = lax.rem(frame + i, FRAMES)
        pltpu.make_async_remote_copy(
            src_ref=stage.at[to],
            dst_ref=x_ref.at[frame],
            send_sem=send_sem.at[2],
            recv_sem=recv_sem.at[2],
            device_id={"ka": base + 2 * to},
            device_id_type=MESH,
        ).start()
        return 0

    lax.fori_loop(1, FRAMES, hand_on, 0)
    x_ref[frame] = stage[frame]
    words = word_ref.at[pl.ds(0, count - 1)]
    pltpu.make_async_copy(words, words, recv_sem.at[1]).wait()
    rest = x_ref.at[pl.ds(0, FRAMES - 1)]
    pltpu.make_async_copy(rest, rest, recv_sem.at[2]).wait()
    pltpu.make_async_copy(most, most, send_sem.at[0]).wait()
    pltpu.make_async_copy(words, words, send_sem.at[1]).wait()
    pltpu.make_async_copy(rest, rest, send_sem.at[2]).wait()


def call_spread(plan, k_index, positions):
    smem = pl.BlockSpec(memory_space=pltpu.SMEM)
    vmem = pl.BlockSpec(memory_space=pltpu.VMEM)
    count = lax.axis_size("ka")
    rows = positions.shape[2] // (128 * count)
    positions = positions.reshape(3, rows * count, 128)
    return pl.pallas_call(
        spread_kernel,
        out_shape=(
            jax.ShapeDtypeStruct((FRAMES, 3, rows, 128), f32),
            jax.ShapeDtypeStruct((count, 1, k_index.shape[1]), jnp.int32),
        ),
        in_specs=[smem, vmem, pl.BlockSpec(memory_space=pl.ANY)],
        out_specs=(vmem, vmem),
        scratch_shapes=[
            pltpu.VMEM((count, 3, rows, 128), f32),
            pltpu.VMEM((FRAMES, 3, rows, 128), f32),
            pltpu.VMEM((1, k_index.shape[1]), jnp.int32),
            pltpu.SemaphoreType.DMA((3,)),
            pltpu.SemaphoreType.DMA((3,)),
            pltpu.SemaphoreType.DMA,
        ],
        compiler_params=pltpu.CompilerParams(collective_id=0, has_side_effects=True),
    )(plan, k_index, positions)


def pick_blocks(grid, pick, word_ref, modes, blocks):
    lanes = lax.broadcasted_iota(jnp.int32, (8, 128), 1)
    upper = lax.broadcasted_iota(jnp.int32, (8, 128), 0) < 4
    for b in blocks:
        found = jnp.zeros((8, 128), f32)
        for j in range(128):
            word = pick[b, 0, j]
            found = jnp.where(lanes == j, pltpu.roll(grid[word >> 8], word & 127, axis=1), found)
        sign = jnp.where((word_ref[b] & 128) > 0, -1.0, 1.0)
        modes[b] = found * jnp.where(upper, 1.0, sign)


def factors_kernel(scale, grid, word_ref, out_ref, modes, parts, pick, send_sem, recv_sem, own_sem):
    me = lax.axis_index("ka")
    half = lax.axis_index("atoms")
    count = lax.axis_size("ka")
    barrier = pltpu.get_barrier_semaphore()
    fetch = pltpu.make_async_copy(word_ref, pick, own_sem)
    fetch.start()

    def greet(i, _):
        to = lax.rem(me + i, count)
        pl.semaphore_signal(barrier, inc=1, device_id={"ka": to, "atoms": 1 - half}, device_id_type=MESH)

        @pl.when(i < count)
        def _():
            pl.semaphore_signal(barrier, inc=1, device_id={"ka": to, "atoms": half}, device_id_type=MESH)
        return 0

    lax.fori_loop(1, count + 1, greet, 0)
    fetch.wait()
    slot = half * count + me

    def send(i):
        to = lax.rem(me + i + 1, count)

        def copy(h):
            return pltpu.make_async_remote_copy(
                src_ref=modes.at[to],
                dst_ref=parts.at[slot],
                send_sem=send_sem,
                recv_sem=recv_sem,
                device_id={"ka": to, "atoms": h},
                device_id_type=MESH,
            )

        copy(1 - half).start()

        @pl.when(i < count - 1)
        def _():
            copy(half).start()

    def group(g, _):
        pick_blocks(grid, pick, word_ref, modes, [lax.rem(me + GROUP * g + u + 1, count) for u in range(GROUP)])

        @pl.when(g == 1)
        def _():
            pl.semaphore_wait(barrier, 2 * count - 1)
            for u in range(GROUP):
                send(u)

        @pl.when(g > 0)
        def _():
            for u in range(GROUP):
                send(GROUP * g + u)
        return 0

    lax.fori_loop(0, count // GROUP, group, 0)
    parts[slot] = modes[me]
    most = parts.at[pl.ds(0, 2 * count - 1)]
    pltpu.make_async_copy(most, most, recv_sem).wait()
    window = []
    for f in range(FRAMES):
        total = None
        for high in range(2 * count // 16):
            for core in range(2):
                part = parts[high * 16 + f * 2 + core]
                total = part if total is None else total + part
        window.append(total)
    upper = lax.broadcasted_iota(jnp.int32, (8, 128), 0) < 4
    crossed = [jnp.where(upper, 1.0, -1.0) * pltpu.roll(w, 4, axis=0) for w in window]
    pairs = ((0, 0), (0, 1), (0, 2), (1, 1), (1, 2), (2, 2))
    for f in range(FRAMES):
        wave = window[0]
        for t in range(1, FRAMES):
            turn = 2 * math.pi * (f * t % FRAMES) / FRAMES
            wave = wave + math.cos(turn) * window[t] + math.sin(turn) * crossed[t]
        for p, (a, b) in enumerate(pairs):
            value = wave[a:a + 1] * wave[b:b + 1] + wave[4 + a:5 + a] * wave[4 + b:5 + b]
            out_ref[f, p:p + 1] = value * scale
    pltpu.make_async_copy(most, most, send_sem).wait()


def call_factors(grid, words, total_atoms):
    vmem = pl.BlockSpec(memory_space=pltpu.VMEM)
    count = lax.axis_size("ka")
    lanes = words.shape[2]
    return pl.pallas_call(
        functools.partial(factors_kernel, 1.0 / (FRAMES * total_atoms)),
        out_shape=jax.ShapeDtypeStruct((FRAMES, 6, lanes), f32),
        in_specs=[vmem, vmem],
        out_specs=vmem,
        scratch_shapes=[
            pltpu.VMEM((count, 8, lanes), f32),
            pltpu.VMEM((2 * count, 8, lanes), f32),
            pltpu.SMEM(words.shape, jnp.int32),
            pltpu.SemaphoreType.DMA,
            pltpu.SemaphoreType.DMA,
            pltpu.SemaphoreType.DMA,
        ],
        compiler_params=pltpu.CompilerParams(collective_id=1, has_side_effects=True, vmem_limit_bytes=20 * 1024 * 1024),
    )(grid.reshape(13 * LINES, 8, 128), words)


def local(positions, counts, plan, k_index):
    me = lax.axis_index("ka")
    x, words = call_spread(plan, k_index, positions)
    first = me - lax.rem(me // 2, FRAMES) * 2
    grid = call_lattice(counts, first.astype(jnp.int32).reshape(1), x)
    return call_factors(grid, words, positions.shape[2] * lax.axis_size("atoms"))


def solution(mesh):
    return jax.shard_map(
        local,
        mesh=mesh,
        in_specs=(P("ka", None, "atoms"), P("atoms", None), P(), P(None, "ka")),
        out_specs=P(None, None, "ka"),
        check_vma=False,
    )
```

time: 92.3 us -> 66.6 us (0.72)
  Pallas kernels: 87.6 us -> 64.4 us
  local copies, waits for them, and re-layouts: 4.26 us -> 2.06 us
    pallas_call x1, Pallas kernels: 47.6 us -> 17.3 us  [call_lattice(): pl.pallas_call(lattice_kernel, out_shape=jax.ShapeDtypeStruct((13 * LINES...]
    pallas_call x1, Pallas kernels: 19.4 us -> 26.4 us  [call_factors(): pl.pallas_call(functools.partial(factors_kernel, 1.0 / (FRAMES * total_at...]
    unnamed x8 -> x6, local copies, waits for them, and re-layouts: 2.89 us -> 1.45 us
where the time goes in v3:
time: 66.6 us; the launch traced here: 66.5 us
  Pallas kernels  64.4 us (97%)
  local copies, waits for them, and re-layouts  2.06 us (3%)
    pallas_call x1, Pallas kernels, call_factors(): pl.pallas_call(functools.partial(factors_kernel, 1.0 / (FRAMES * total_at...  26.4 us
    pallas_call x1, Pallas kernels, call_spread(): pl.pallas_call(spread_kernel, out_shape=(jax.ShapeDtypeStruct((FRAMES, 3,...  20.6 us
    pallas_call x1, Pallas kernels, call_lattice(): pl.pallas_call(lattice_kernel, out_shape=jax.ShapeDtypeStruct((13 * LINES...  17.3 us
    unnamed x6, local copies, waits for them, and re-layouts  1.45 us

profile of v3, /device:TPU:1, one launch (start us, length us, event | category | flops | bytes accessed | tf_op | source)
XLA Modules:
  0.0 66.5 jit_solution(6905339802262202200)
XLA Ops:
  0.0 20.6 %shard_map.46 = (f32[8,3,4,128]{3,2,1,0:T(4,128)}, s32[64,1,128]{2,1,0:T(1,128)}) custom-call(s32[8]{0:T(128)} %plan.1, s32[3,128]{1,0:T(4,128)} %k_ref.1, f32[3,256,128]{2,1,0:T(8,128)} %bitcast.4), custom_call_target="tpu_custom_call" | custom-call | tf_op jit(solution)/shard_map/pallas_call | solution.py:257
  20.6 0.0 copy-start
  20.6 0.8 %copy-done = f32[8,3,4,128]{3,2,1,0:T(4,128)S(1)} copy-done((f32[8,3,4,128]{3,2,1,0:T(4,128)S(1)}, f32[8,3,4,128]{3,2,1,0:T(4,128)}, u32[]{:S(2)}) %copy-start) | copy-done | bytes 49176
  21.4 0.0 copy-start.2
  21.4 0.7 copy-done.2
  22.1 0.0 copy-start.1
  22.1 17.3 %shard_map.47 = f32[9152,128]{1,0:T(8,128)S(1)} custom-call(s32[1,3]{1,0:T(1,128)S(1)} %copy-done.2, s32[1]{0:T(128)} %bitcast.base, f32[8,3,4,128]{3,2,1,0:T(4,128)S(1)} %copy-done), custom_call_target="tpu_custom_call" | custom-call | tf_op jit(solution)/shard_map/pallas_call | solution.py:151
  39.4 0.0 copy-done.1
  39.4 26.4 %shard_map.48 = f32[8,6,128]{2,1,0:T(8,128)S(1)} custom-call(f32[1144,8,128]{2,1,0:T(8,128)S(1)} %bitcast.3, s32[64,1,128]{2,1,0:T(1,128)S(1)} %copy-done.1), custom_call_target="tpu_custom_call" | custom-call | tf_op jit(solution)/shard_map/pallas_call | solution.py:374
  65.8 0.6 copy.5
Async XLA Ops:
  20.6 0.8 %copy-start = (f32[8,3,4,128]{3,2,1,0:T(4,128)S(1)}, f32[8,3,4,128]{3,2,1,0:T(4,128)}, u32[]{:S(2)}) copy-start(f32[8,3,4,128]{3,2,1,0:T(4,128)} %get-tuple-element.7.x_ref) | copy-start | bytes 147460
  21.4 0.7 copy-start.2
  22.1 17.4 %copy-start.1 = (s32[64,1,128]{2,1,0:T(1,128)S(1)}, s32[64,1,128]{2,1,0:T(1,128)}, u32[]{:S(2)}) copy-start(s32[64,1,128]{2,1,0:T(1,128)} %get-tuple-element.8.word_ref) | copy-start | bytes 98308

commit v4 on v3

v4 whole, which is shorter than its diff:
```python
import functools
import math

import jax
import jax.numpy as jnp
import numpy as np
from jax import lax
from jax.experimental import pallas as pl
from jax.experimental.pallas import tpu as pltpu
from jax.sharding import PartitionSpec as P

MESH = pl.DeviceIdType.MESH
FRAMES = 8
LINES = 88
COARSE = 13
CHUNK = 256
GROUP = 4
HOPS = (0, 1, 2, 1)
ORDER = sorted(
    [(z, y, x, c) for c in range(2) for x in range(4) for y in range(4) for z in range(2) if z + y + x + c],
    key=lambda d: -(d[0] + HOPS[d[1]] + HOPS[d[2]]),
)
f32 = jnp.float32
bf16 = jnp.bfloat16

def fit_coefs():
    t = np.cos(np.pi * (np.arange(4000) + 0.5) / 4000) * 0.5
    u = t * t
    a = np.vander(u, 5, increasing=True)
    ps = np.linalg.lstsq(a * t[:, None], np.sin(np.pi * t), rcond=None)[0]
    pc = np.linalg.lstsq(a, np.cos(np.pi * t), rcond=None)[0]
    return [float(x) for x in ps], [float(x) for x in pc]

SIN_C, COS_C = fit_coefs()

def waves(cycles):
    t = cycles - jnp.round(cycles)
    u = t * t
    s = jnp.full_like(u, SIN_C[-1])
    for c in SIN_C[-2::-1]:
        s = s * u + c
    s = s * t
    q = jnp.full_like(u, COS_C[-1])
    for c in COS_C[-2::-1]:
        q = q * u + c
    twice = s + s
    return 1.0 - twice * s, twice * q

def split(x):
    hi = x.astype(bf16)
    lo = (x - hi.astype(f32)).astype(bf16)
    return hi, lo

def balanced(index, base, reach, mul, shift, below=0):
    upper = (((index + reach + base * below) * mul) >> shift) - below
    return upper, index - base * upper

def lattice_kernel(counts_ref, x_ref, grid, e01_a, e01_b, e2_a, e2_b, rhs_a, rhs_b, acc, counts, counts_sem):
    fetch = pltpu.make_async_copy(counts_ref, counts, counts_sem)
    fetch.start()
    me = lax.axis_index("ka")
    base = me - 2 * lax.rem(me // 2, FRAMES)
    acc[...] = jnp.zeros_like(acc)
    fetch.wait()
    pieces, _, rows, _ = x_ref.shape
    piece = rows * 128
    per_piece = piece // CHUNK
    chunks = pieces * per_piece
    end = [counts[0, 0], counts[0, 0] + counts[0, 1]]
    below = []
    for e in end:
        total = 0
        for p in range(pieces):
            total = total + jnp.clip(e - (base + 2 * p) * piece, 0, piece)
        below.append(total)
    cut0, cut1 = below
    turn0 = (cut0 + CHUNK - 1) // CHUNK
    turn1 = turn0 + (cut1 + CHUNK - 1) // CHUNK - cut0 // CHUNK

    lane = lax.broadcasted_iota(jnp.int32, (1, CHUNK), 1)

    def visit(v):
        kind = (v >= turn0).astype(jnp.int32) + (v >= turn1).astype(jnp.int32)
        chunk = jnp.where(kind == 0, v, jnp.where(kind == 1, v - turn0 + cut0 // CHUNK, v - turn1 + cut1 // CHUNK))
        first = jnp.where(kind == 0, 0, jnp.where(kind == 1, cut0, cut1))
        last = jnp.where(kind == 0, cut0, jnp.where(kind == 1, cut1, chunks * CHUNK))
        return kind, chunk, first, last

    def prepare(v, e01, e2, rhs):
        _, chunk, first, last = visit(v)
        here = jnp.minimum(chunk, chunks - 1)
        xs = []
        for d in range(3):
            at = lax.rem(here, per_piece) * (CHUNK // 128)
            parts = [x_ref[here // per_piece, d, pl.ds(at + n, 1)] for n in range(CHUNK // 128)]
            whole = jnp.concatenate(parts, axis=1)
            xs.append(whole - jnp.round(whole))
        where = chunk * CHUNK + lane
        mask = jnp.logical_and(where >= first, where < last).astype(f32)

        def lines(row):
            line = row + lax.broadcasted_iota(jnp.int32, (8, CHUNK), 0)
            q0, q1 = [(5 * q).astype(f32) for q in balanced(line, 13, 6, 79, 10)]
            c, s = waves(q0 * xs[0] + q1 * xs[1])
            e01[row:row + 8] = c
            e01[LINES + row:LINES + row + 8] = s

        def depths():
            q2 = (5 * lax.broadcasted_iota(jnp.int32, (8, CHUNK), 0)).astype(f32)
            c, s = waves(q2 * xs[2])
            e2[0:8] = c
            e2[8:16] = s

        def columns(row):
            index = row + lax.broadcasted_iota(jnp.int32, (16, CHUNK), 0)
            r0, rest = balanced(index, 25, 12, 41, 10)
            r1, r2 = balanced(rest, 5, 2, 205, 10, 3)
            c, s = waves(r0.astype(f32) * xs[0] + r1.astype(f32) * xs[1] + r2.astype(f32) * xs[2])
            for at, value in ((row, c), (64 + row, s)):
                hi, lo = split(value * mask)
                rhs[at:at + 16] = hi
                rhs[128 + at:144 + at] = lo

        steps = [functools.partial(lines, row) for row in range(0, LINES, 8)]
        steps += [functools.partial(columns, row) for row in range(0, 64, 16)]
        return steps + [depths]

    def gather(v, e01, e2, rhs, steps):
        kind = visit(v)[0]
        weights = rhs[...]
        for l in range(0, COARSE, 3):
            some = range(l, min(l + 3, COARSE))
            parts = []
            for m in some:
                row = m if m < 7 else m + 2
                parts += split(e01[...] * e2[row:row + 1])
            lhs = jnp.concatenate(parts, axis=0)
            p = lax.dot_general(lhs, weights, (((1,), (1,)), ((), ())), preferred_element_type=f32)
            for m in some:
                at = (m - l) * 4 * LINES
                one = p[at:at + 2 * LINES] + p[at + 2 * LINES:at + 4 * LINES]
                acc[kind, m] += one[:, :128] + one[:, 128:]
            for step in steps[l * len(steps) // COARSE:min(l + 3, COARSE) * len(steps) // COARSE]:
                step()

    buffers = ((e01_a, e2_a, rhs_a), (e01_b, e2_b, rhs_b))
    for step in prepare(0, *buffers[0]):
        step()

    def pair(i, _):
        gather(2 * i, *buffers[0], prepare(2 * i + 1, *buffers[1]))
        gather(2 * i + 1, *buffers[1], prepare(2 * i + 2, *buffers[0]))
        return 0

    lax.fori_loop(0, (chunks + 2) // 2, pair, 0)

    front = lax.broadcasted_iota(jnp.int32, (LINES, 128), 1) < 64

    def put(q2, sp, a, b):
        plus = b + pltpu.roll(a, 64, axis=1)
        minus = a - pltpu.roll(b, 64, axis=1)
        at = (q2 + 6) * LINES * 8 + sp
        grid[pl.ds(at, LINES, stride=8), :] = jnp.where(front, minus, plus)
        grid[pl.ds(at + 4, LINES, stride=8), :] = jnp.where(front, plus, -minus)

    for sp in range(3):
        put(0, sp, acc[sp, 0, 0:LINES], acc[sp, 0, LINES:])
        for l in range(1, 7):
            cc, sc = acc[sp, l, 0:LINES], acc[sp, l, LINES:]
            cs, ss = acc[sp, l + 6, 0:LINES], acc[sp, l + 6, LINES:]
            put(l, sp, cc - ss, sc + cs)
            put(-l, sp, cc + ss, sc - cs)


def call_lattice(counts, x):
    vmem = pl.BlockSpec(memory_space=pltpu.VMEM)
    return pl.pallas_call(
        lattice_kernel,
        out_shape=jax.ShapeDtypeStruct((13 * LINES * 8, 128), f32),
        in_specs=[vmem, vmem],
        out_specs=vmem,
        scratch_shapes=[pltpu.VMEM((2 * LINES, CHUNK), f32)] * 2
        + [pltpu.VMEM((16, CHUNK), f32)] * 2
        + [pltpu.VMEM((256, CHUNK), bf16)] * 2
        + [pltpu.VMEM((3, COARSE, 2 * LINES, 128), f32), pltpu.SMEM(counts.shape, jnp.int32), pltpu.SemaphoreType.DMA],
        compiler_params=pltpu.CompilerParams(vmem_limit_bytes=24 * 1024 * 1024),
    )(counts, x)


def picks(k_index):
    n = [k_index[d:d + 1] for d in range(3)]
    q, r = zip(*[balanced(v, 5, 2, 205, 10, 6) for v in n])
    jc = 13 * q[0] + q[1]
    sq = jnp.where(jc < 0, 1, 0)
    tile = (jnp.where(jc < 0, -q[2], q[2]) + 6) * LINES + jnp.abs(jc)
    rc = 25 * r[0] + 5 * r[1] + r[2]
    sr = jnp.where(rc < 0, 1, 0)
    lane = lax.broadcasted_iota(jnp.int32, rc.shape, 1)
    shift = (lane - jnp.abs(rc) - 64 * (sr ^ sq)) & 127
    return tile * 256 + sq * 128 + shift


def spread_kernel(small_ref, pos_ref, x_ref, word_ref, bound_ref, slots, stage, plan, send_sem, recv_sem, own_sem):
    me = lax.axis_index("ka")
    count = lax.axis_size("ka")
    frame = lax.rem(me // 2, FRAMES)
    base = me - 2 * frame
    wide = 2 * FRAMES
    groups = count // FRAMES
    mine = me // wide * 2 + lax.rem(me, 2)
    barrier = pltpu.get_barrier_semaphore()
    fetches = [
        pltpu.make_async_copy(small_ref, plan, own_sem.at[0]),
        pltpu.make_async_copy(pos_ref.at[:, me], slots.at[me], own_sem.at[1]),
    ]
    for fetch in fetches:
        fetch.start()

    def greet(i, _):
        pl.semaphore_signal(barrier, inc=1, device_id={"ka": lax.rem(me + i, count)}, device_id_type=MESH)
        return 0

    lax.fori_loop(1, count, greet, 0)
    bound_ref[...] = small_ref[3:4]
    word_ref[mine, pl.ds(frame, 1)] = picks(small_ref[0:3])
    pl.semaphore_wait(barrier, count - 1)

    def share(i, _):
        to = lax.rem(frame + i, FRAMES)
        pltpu.make_async_remote_copy(
            src_ref=word_ref.at[mine, pl.ds(frame, 1)],
            dst_ref=word_ref.at[mine, pl.ds(frame, 1)],
            send_sem=send_sem.at[1],
            recv_sem=recv_sem.at[1],
            device_id={"ka": base + 2 * to},
            device_id_type=MESH,
        ).start()
        return 0

    lax.fori_loop(1, FRAMES, share, 0)

    z, y, x, core = me // 32, lax.rem(me // 8, 4), lax.rem(me // 2, 4), lax.rem(me, 2)
    for dz, dy, dx, dc in ORDER:
        to = lax.rem(z + dz, 2) * 32 + lax.rem(y + dy, 4) * 8 + lax.rem(x + dx, 4) * 2 + lax.rem(core + dc, 2)
        pltpu.make_async_remote_copy(
            src_ref=pos_ref.at[:, to],
            dst_ref=slots.at[me],
            send_sem=send_sem.at[0],
            recv_sem=recv_sem.at[0],
            device_id={"ka": to},
            device_id_type=MESH,
        ).start()
    row = word_ref.at[mine, pl.ds(0, FRAMES - 1)]
    pltpu.make_async_copy(row, row, recv_sem.at[1]).wait()

    def share_group(i, _):
        to = lax.rem(mine + i, groups)
        pltpu.make_async_remote_copy(
            src_ref=word_ref.at[mine],
            dst_ref=word_ref.at[mine],
            send_sem=send_sem.at[3],
            recv_sem=recv_sem.at[3],
            device_id={"ka": to // 2 * wide + 2 * frame + lax.rem(to, 2)},
            device_id_type=MESH,
        ).start()
        return 0

    lax.fori_loop(1, groups, share_group, 0)
    for fetch in fetches:
        fetch.wait()
    most = slots.at[pl.ds(0, count - 1)]
    pltpu.make_async_copy(most, most, recv_sem.at[0]).wait()
    for f in range(FRAMES):
        stage[f] = slots[plan[3, 8 + f]]

    def hand_on(i, _):
        to = lax.rem(frame + i, FRAMES)
        pltpu.make_async_remote_copy(
            src_ref=stage.at[to],
            dst_ref=x_ref.at[frame],
            send_sem=send_sem.at[2],
            recv_sem=recv_sem.at[2],
            device_id={"ka": base + 2 * to},
            device_id_type=MESH,
        ).start()
        return 0

    lax.fori_loop(1, FRAMES, hand_on, 0)
    x_ref[frame] = stage[frame]
    words = word_ref.at[pl.ds(0, groups - 1)]
    rest = x_ref.at[pl.ds(0, FRAMES - 1)]
    pltpu.make_async_copy(words, words, recv_sem.at[3]).wait()
    pltpu.make_async_copy(most, most, send_sem.at[0]).wait()
    pltpu.make_async_copy(row, row, send_sem.at[1]).wait()
    pltpu.make_async_copy(words, words, send_sem.at[3]).wait()
    pltpu.make_async_copy(rest, rest, recv_sem.at[2]).wait()
    pltpu.make_async_copy(rest, rest, send_sem.at[2]).wait()


def call_spread(plan, k_index, counts, positions):
    hbm = pl.BlockSpec(memory_space=pltpu.HBM)
    vmem = pl.BlockSpec(memory_space=pltpu.VMEM)
    count = lax.axis_size("ka")
    rows = positions.shape[2] // (128 * count)
    lanes = k_index.shape[1]
    small = jnp.pad(k_index, ((0, 1), (0, 0))) + jnp.pad(counts, ((3, 0), (0, lanes - 3))) + jnp.pad(plan[None], ((3, 0), (8, lanes - 16)))
    return pl.pallas_call(
        spread_kernel,
        out_shape=(
            jax.ShapeDtypeStruct((FRAMES, 3, rows, 128), f32),
            jax.ShapeDtypeStruct((count // FRAMES, FRAMES, lanes), jnp.int32),
            jax.ShapeDtypeStruct((1, lanes), jnp.int32),
        ),
        in_specs=[vmem, hbm],
        out_specs=(vmem, vmem, vmem),
        scratch_shapes=[
            pltpu.VMEM((count, 3, rows, 128), f32),
            pltpu.VMEM((FRAMES, 3, rows, 128), f32),
            pltpu.SMEM((4, lanes), jnp.int32),
            pltpu.SemaphoreType.DMA((4,)),
            pltpu.SemaphoreType.DMA((4,)),
            pltpu.SemaphoreType.DMA((2,)),
        ],
        compiler_params=pltpu.CompilerParams(collective_id=0, has_side_effects=True, vmem_limit_bytes=8 * 1024 * 1024),
    )(small, positions.reshape(3, count, rows, 128))


def pick_blocks(grid, pick, word_ref, modes, blocks, places):
    lanes = lax.broadcasted_iota(jnp.int32, (8, 128), 1)
    upper = lax.broadcasted_iota(jnp.int32, (8, 128), 0) < 4
    for b, at in zip(blocks, places):
        group, lead = b // (2 * FRAMES) * 2 + lax.rem(b, 2), lax.rem(b // 2, FRAMES)
        found = jnp.zeros((8, 128), f32)
        for j in range(128):
            word = pick[group, lead, j]
            found = jnp.where(lanes == j, pltpu.roll(grid[word >> 8], word & 127, axis=1), found)
        sign = jnp.where((word_ref[group, pl.ds(lead, 1)] & 128) > 0, -1.0, 1.0)
        modes[at] = found * jnp.where(upper, 1.0, sign)


def factors_kernel(scale, grid, word_ref, out_ref, modes, spare, parts, beside, pick, send_sem, recv_sem, own_sem):
    me = lax.axis_index("ka")
    half = lax.axis_index("atoms")
    chips = lax.axis_size("ka") // 2
    chip, core = me // 2, lax.rem(me, 2)
    barrier = pltpu.get_barrier_semaphore()
    fetch = pltpu.make_async_copy(word_ref, pick, own_sem)
    fetch.start()

    def greet(i, _):
        to = 2 * lax.rem(chip + i, chips) + core
        pl.semaphore_signal(barrier, inc=1, device_id={"ka": to, "atoms": 1 - half}, device_id_type=MESH)

        @pl.when(i < chips)
        def _():
            pl.semaphore_signal(barrier, inc=1, device_id={"ka": to, "atoms": half}, device_id_type=MESH)
        return 0

    pl.semaphore_signal(barrier, inc=1, device_id={"ka": 2 * chip + 1 - core}, device_id_type=MESH)
    lax.fori_loop(1, chips + 1, greet, 0)
    fetch.wait()
    slot = half * chips + chip

    def place(i):
        return lax.rem(chip + i + 1, chips)

    def hand_over(g):
        pltpu.make_async_remote_copy(
            src_ref=spare.at[pl.ds(GROUP * g, GROUP)],
            dst_ref=beside.at[pl.ds(GROUP * g, GROUP)],
            send_sem=send_sem.at[0],
            recv_sem=recv_sem.at[0],
            device_id={"ka": 2 * chip + 1 - core},
            device_id_type=MESH,
        ).start()

    def first_half(g, _):
        at = [GROUP * g + u for u in range(GROUP)]
        pick_blocks(grid, pick, word_ref, spare, [2 * place(i) + 1 - core for i in at], at)

        @pl.when(g == 1)
        def _():
            pl.semaphore_wait(barrier, 2 * chips)
            hand_over(0)

        @pl.when(g > 0)
        def _():
            hand_over(g)
        return 0

    lax.fori_loop(0, chips // GROUP, first_half, 0)
    handed = beside.at[pl.ds(0, chips)]

    def send(i):
        to = place(i)
        modes[i] += beside[i]

        def copy(h):
            return pltpu.make_async_remote_copy(
                src_ref=modes.at[i],
                dst_ref=parts.at[slot],
                send_sem=send_sem.at[1],
                recv_sem=recv_sem.at[1],
                device_id={"ka": 2 * to + core, "atoms": h},
                device_id_type=MESH,
            )

        copy(1 - half).start()

        @pl.when(i < chips - 1)
        def _():
            copy(half).start()

    def second_half(g, _):
        at = [GROUP * g + u for u in range(GROUP)]
        pick_blocks(grid, pick, word_ref, modes, [2 * place(i) + core for i in at], at)

        @pl.when(g == 1)
        def _():
            pltpu.make_async_copy(handed, handed, recv_sem.at[0]).wait()
            for u in range(GROUP):
                send(u)

        @pl.when(g > 0)
        def _():
            for i in at:
                send(i)
        return 0

    lax.fori_loop(0, chips // GROUP, second_half, 0)
    parts[slot] = modes[chips - 1]
    most = parts.at[pl.ds(0, 2 * chips - 1)]
    pltpu.make_async_copy(most, most, recv_sem.at[1]).wait()
    window = []
    for f in range(FRAMES):
        total = None
        for high in range(2 * chips // FRAMES):
            part = parts[high * FRAMES + f]
            total = part if total is None else total + part
        window.append(total)
    upper = lax.broadcasted_iota(jnp.int32, (8, 128), 0) < 4
    crossed = [jnp.where(upper, 1.0, -1.0) * pltpu.roll(w, 4, axis=0) for w in window]
    pairs = ((0, 0), (0, 1), (0, 2), (1, 1), (1, 2), (2, 2))
    for f in range(FRAMES):
        wave = window[0]
        for t in range(1, FRAMES):
            turn = 2 * math.pi * (f * t % FRAMES) / FRAMES
            wave = wave + math.cos(turn) * window[t] + math.sin(turn) * crossed[t]
        for p, (a, b) in enumerate(pairs):
            value = wave[a:a + 1] * wave[b:b + 1] + wave[4 + a:5 + a] * wave[4 + b:5 + b]
            out_ref[p, f:f + 1] = value * scale
    pltpu.make_async_copy(handed, handed, send_sem.at[0]).wait()
    pltpu.make_async_copy(most, most, send_sem.at[1]).wait()


def call_factors(grid, words, total_atoms):
    vmem = pl.BlockSpec(memory_space=pltpu.VMEM)
    count = lax.axis_size("ka")
    lanes = words.shape[2]
    return pl.pallas_call(
        functools.partial(factors_kernel, 1.0 / (FRAMES * total_atoms)),
        out_shape=jax.ShapeDtypeStruct((6, FRAMES, lanes), f32),
        in_specs=[vmem, vmem],
        out_specs=vmem,
        scratch_shapes=[
            pltpu.VMEM((count // 2, 8, lanes), f32),
            pltpu.VMEM((count // 2, 8, lanes), f32),
            pltpu.VMEM((count, 8, lanes), f32),
            pltpu.VMEM((count // 2 + 1, 8, lanes), f32),
            pltpu.SMEM(words.shape, jnp.int32),
            pltpu.SemaphoreType.DMA((2,)),
            pltpu.SemaphoreType.DMA((2,)),
            pltpu.SemaphoreType.DMA,
        ],
        compiler_params=pltpu.CompilerParams(collective_id=1, has_side_effects=True, vmem_limit_bytes=20 * 1024 * 1024),
    )(grid.reshape(13 * LINES, 8, 128), words)


def local(positions, counts, plan, k_index):
    x, words, bounds = call_spread(plan, k_index, counts, positions)
    grid = call_lattice(bounds, x)
    factors = call_factors(grid, words, positions.shape[2] * lax.axis_size("atoms"))
    return jnp.transpose(factors, (1, 0, 2))


def solution(mesh):
    return jax.shard_map(
        local,
        mesh=mesh,
        in_specs=(P("ka", None, "atoms"), P("atoms", None), P(), P(None, "ka")),
        out_specs=P(None, None, "ka"),
        check_vma=False,
    )
```

time: 66.6 us -> 62.3 us (0.935)
  Pallas kernels: 64.4 us -> 59.4 us
  other arithmetic: 0 us -> 0.79 us
    pallas_call x1, Pallas kernels: 20.6 us -> 18.4 us  [call_spread(): pl.pallas_call(spread_kernel, out_shape=(jax.ShapeDtypeStruct((FRAMES, 3,...]
    pallas_call x1, Pallas kernels: 26.4 us -> 24.5 us  [call_factors(): pl.pallas_call(functools.partial(factors_kernel, 1.0 / (FRAMES * total_at...]
    add x0 -> x1, other arithmetic: none -> 0.79 us  [call_spread(): jnp.pad(k_index, ((0, 1), (0, 0)))]
    pallas_call x1, Pallas kernels: 17.3 us -> 16.6 us  [call_lattice(): pl.pallas_call(lattice_kernel, out_shape=jax.ShapeDtypeStruct((13 * LINES...]
    unnamed x6 -> x3, local copies, waits for them, and re-layouts: 1.45 us -> 1.61 us
where the time goes in v4:
time: 62.3 us; the launch traced here: 61.8 us
  Pallas kernels  59.4 us (95%)
  local copies, waits for them, and re-layouts  1.61 us (3%)
  other arithmetic  0.79 us (1%)
    pallas_call x1, Pallas kernels, call_factors(): pl.pallas_call(functools.partial(factors_kernel, 1.0 / (FRAMES * total_at...  24.5 us
    pallas_call x1, Pallas kernels, call_spread(): pl.pallas_call(spread_kernel, out_shape=(jax.ShapeDtypeStruct((FRAMES, 3,...  18.4 us
    pallas_call x1, Pallas kernels, call_lattice(): pl.pallas_call(lattice_kernel, out_shape=jax.ShapeDtypeStruct((13 * LINES...  16.6 us
    unnamed x3, local copies, waits for them, and re-layouts  1.61 us

profile of v4, /device:TPU:1, one launch (start us, length us, event | category | flops | bytes accessed | tf_op | source)
XLA Modules:
  0.0 61.8 jit_solution(14581708275299871135)
XLA Ops:
  0.0 0.8 %pad_add_fusion.small_ref = s32[4,128]{1,0:T(4,128)S(1)} fusion(s32[1,8]{1,0:T(1,128)} %bitcast.7, s32[1,3]{1,0:T(1,128)} %param.5, s32[3,128]{1,0:T(4,128)} %param.7), kind=kLoop, calls=%fused_computation | loop fusion | flops 1024 | bytes 3628 | tf_op jit(solution)/shard_map/add | solution.py:306
  0.8 0.0 copy-start
  0.8 1.0 %copy-done = f32[1,3,32768]{2,0,1:T(1,128)S(1)} copy-done((f32[1,3,32768]{2,0,1:T(1,128)S(1)}, f32[1,3,32768]{2,0,1:T(1,128)}, u32[]{:S(2)}) %copy-start) | copy-done | bytes 393240
  1.8 18.4 %shard_map.46 = (f32[8,3,4,128]{3,2,1,0:T(4,128)S(1)}, s32[8,8,128]{2,1,0:T(8,128)S(1)}, s32[1,128]{1,0:T(1,128)S(1)}) custom-call(s32[4,128]{1,0:T(4,128)S(1)} %pad_add_fusion.small_ref, f32[3,64,4,128]{3,2,1,0:T(4,128)S(1)} %bitcast.5), custom_call_target="tpu_custom_call" | custom-call | tf_op jit(solution)/shard_map/pallas_call | solution.py:307
  20.2 16.6 %shard_map.47 = f32[9152,128]{1,0:T(8,128)S(1)} custom-call(s32[1,128]{1,0:T(1,128)S(1)} %get-tuple-element.8.counts_ref, f32[8,3,4,128]{3,2,1,0:T(4,128)S(1)} %get-tuple-element.9.x_ref), custom_call_target="tpu_custom_call" | custom-call | tf_op jit(solution)/shard_map/pallas_call | solution.py:177
  36.7 24.5 %shard_map.48 = f32[6,8,128]{2,1,0:T(8,128)S(1)} custom-call(f32[1144,8,128]{2,1,0:T(8,128)S(1)} %bitcast.4, s32[8,8,128]{2,1,0:T(8,128)S(1)} %get-tuple-element.10.word_ref), custom_call_target="tpu_custom_call" | custom-call | tf_op jit(solution)/shard_map/pallas_call | solution.py:460
  61.2 0.6 copy.6
Async XLA Ops:
  0.8 1.0 %copy-start = (f32[1,3,32768]{2,0,1:T(1,128)S(1)}, f32[1,3,32768]{2,0,1:T(1,128)}, u32[]{:S(2)}) copy-start(f32[1,3,32768]{2,0,1:T(1,128)} %param.4) | copy-start | bytes 1179652

commit v5 on v4

--- a/solution.py
+++ b/solution.py
@@ -76,6 +76,7 @@
     cut0, cut1 = below
     turn0 = (cut0 + CHUNK - 1) // CHUNK
     turn1 = turn0 + (cut1 + CHUNK - 1) // CHUNK - cut0 // CHUNK
+    visits = turn1 + chunks - cut1 // CHUNK
 
     lane = lax.broadcasted_iota(jnp.int32, (1, CHUNK), 1)
 
@@ -152,7 +153,17 @@
         gather(2 * i + 1, *buffers[1], prepare(2 * i + 2, *buffers[0]))
         return 0
 
-    lax.fori_loop(0, (chunks + 2) // 2, pair, 0)
+    lax.fori_loop(0, chunks // 2, pair, 0)
+
+    @pl.when(visits > chunks)
+    def _():
+        gather(chunks, *buffers[0], [])
+
+    @pl.when(visits > chunks + 1)
+    def _():
+        for step in prepare(chunks + 1, *buffers[1]):
+            step()
+        gather(chunks + 1, *buffers[1], [])
 
     front = lax.broadcasted_iota(jnp.int32, (LINES, 128), 1) < 64
 
@@ -321,7 +332,7 @@
             pltpu.SemaphoreType.DMA((4,)),
             pltpu.SemaphoreType.DMA((2,)),
         ],
-        compiler_params=pltpu.CompilerParams(collective_id=0, has_side_effects=True, vmem_limit_bytes=8 * 1024 * 1024),
+        compiler_params=pltpu.CompilerParams(collective_id=0, has_side_effects=True, vmem_limit_bytes=55000 * 1024),
     )(small, positions.reshape(3, count, rows, 128))
 
 

time: 62.3 us -> 60.9 us (0.978)
  local copies, waits for them, and re-layouts: 1.61 us -> 0.61 us
    pallas_call x1, Pallas kernels: 16.6 us -> 15 us  [call_lattice(): pl.pallas_call(lattice_kernel, out_shape=jax.ShapeDtypeStruct((13 * LINES...]
    unnamed x3 -> x1, local copies, waits for them, and re-layouts: 1.61 us -> 0.61 us
    pallas_call x1, Pallas kernels: 24.5 us -> 25.2 us  [call_factors(): pl.pallas_call(functools.partial(factors_kernel, 1.0 / (FRAMES * total_at...]
where the time goes in v5:
time: 60.9 us; the launch traced here: 60.3 us
  Pallas kernels  58.9 us (97%)
  other arithmetic  0.79 us (1%)
  local copies, waits for them, and re-layouts  0.61 us (1%)
    pallas_call x1, Pallas kernels, call_factors(): pl.pallas_call(functools.partial(factors_kernel, 1.0 / (FRAMES * total_at...  25.2 us
    pallas_call x1, Pallas kernels, call_spread(): pl.pallas_call(spread_kernel, out_shape=(jax.ShapeDtypeStruct((FRAMES, 3,...  18.7 us
    pallas_call x1, Pallas kernels, call_lattice(): pl.pallas_call(lattice_kernel, out_shape=jax.ShapeDtypeStruct((13 * LINES...  15 us

profile of v5, /device:TPU:1, one launch (start us, length us, event | category | flops | bytes accessed | tf_op | source)
XLA Modules:
  0.0 60.3 jit_solution(3021464470580448556)
XLA Ops:
  0.0 0.8 %pad_add_fusion.small_ref = s32[4,128]{1,0:T(4,128)S(1)} fusion(s32[1,8]{1,0:T(1,128)} %bitcast.7, s32[1,3]{1,0:T(1,128)} %param.5, s32[3,128]{1,0:T(4,128)} %param.7), kind=kLoop, calls=%fused_computation | loop fusion | flops 1024 | bytes 3628 | tf_op jit(solution)/shard_map/add | solution.py:317
  0.8 18.7 %shard_map.46 = (f32[8,3,4,128]{3,2,1,0:T(4,128)S(1)}, s32[8,8,128]{2,1,0:T(8,128)S(1)}, s32[1,128]{1,0:T(1,128)S(1)}) custom-call(s32[4,128]{1,0:T(4,128)S(1)} %pad_add_fusion.small_ref, f32[3,64,4,128]{3,2,1,0:T(4,128)} %bitcast.6), custom_call_target="tpu_custom_call" | custom-call | tf_op jit(solution)/shard_map/pallas_call | solution.py:318
  19.5 15.0 %shard_map.47 = f32[9152,128]{1,0:T(8,128)S(1)} custom-call(s32[1,128]{1,0:T(1,128)S(1)} %get-tuple-element.8.counts_ref, f32[8,3,4,128]{3,2,1,0:T(4,128)S(1)} %get-tuple-element.9.x_ref), custom_call_target="tpu_custom_call" | custom-call | tf_op jit(solution)/shard_map/pallas_call | solution.py:188
  34.5 25.2 %shard_map.48 = f32[6,8,128]{2,1,0:T(8,128)S(1)} custom-call(f32[1144,8,128]{2,1,0:T(8,128)S(1)} %bitcast.4, s32[8,8,128]{2,1,0:T(8,128)S(1)} %get-tuple-element.10.word_ref), custom_call_target="tpu_custom_call" | custom-call | tf_op jit(solution)/shard_map/pallas_call | solution.py:471
  59.7 0.6 %copy.6 = f32[8,6,128]{2,0,1:T(8,128)} copy(f32[8,6,128]{2,0,1:T(8,128)S(1)} %bitcast.5) | data formatting | bytes 49152

commit v6 on v5

--- a/solution.py
+++ b/solution.py
@@ -15,6 +15,7 @@
 COARSE = 13
 CHUNK = 256
 GROUP = 4
+BATCH = 16
 HOPS = (0, 1, 2, 1)
 ORDER = sorted(
     [(z, y, x, c) for c in range(2) for x in range(4) for y in range(4) for z in range(2) if z + y + x + c],
@@ -377,8 +378,8 @@
 
     def hand_over(g):
         pltpu.make_async_remote_copy(
-            src_ref=spare.at[pl.ds(GROUP * g, GROUP)],
-            dst_ref=beside.at[pl.ds(GROUP * g, GROUP)],
+            src_ref=spare.at[pl.ds(BATCH * g, BATCH)],
+            dst_ref=beside.at[pl.ds(BATCH * g, BATCH)],
             send_sem=send_sem.at[0],
             recv_sem=recv_sem.at[0],
             device_id={"ka": 2 * chip + 1 - core},
@@ -386,7 +387,7 @@
         ).start()
 
     def first_half(g, _):
-        at = [GROUP * g + u for u in range(GROUP)]
+        at = [BATCH * g + u for u in range(BATCH)]
         pick_blocks(grid, pick, word_ref, spare, [2 * place(i) + 1 - core for i in at], at)
 
         @pl.when(g == 1)
@@ -399,7 +400,7 @@
             hand_over(g)
         return 0
 
-    lax.fori_loop(0, chips // GROUP, first_half, 0)
+    lax.fori_loop(0, chips // BATCH, first_half, 0)
     handed = beside.at[pl.ds(0, chips)]
 
     def send(i):

time: 60.9 us -> 58.4 us (0.959)
  Pallas kernels: 58.9 us -> 56.8 us
    pallas_call x1, Pallas kernels: 25.2 us -> 23.1 us  [call_factors(): pl.pallas_call(functools.partial(factors_kernel, 1.0 / (FRAMES * total_at...]
where the time goes in v6:
time: 58.4 us; the launch traced here: 58.3 us
  Pallas kernels  56.8 us (97%)
  other arithmetic  0.79 us (1%)
  local copies, waits for them, and re-layouts  0.61 us (1%)
    pallas_call x1, Pallas kernels, call_factors(): pl.pallas_call(functools.partial(factors_kernel, 1.0 / (FRAMES * total_at...  23.1 us
    pallas_call x1, Pallas kernels, call_spread(): pl.pallas_call(spread_kernel, out_shape=(jax.ShapeDtypeStruct((FRAMES, 3,...  18.7 us
    pallas_call x1, Pallas kernels, call_lattice(): pl.pallas_call(lattice_kernel, out_shape=jax.ShapeDtypeStruct((13 * LINES...  15 us

profile of v6, /device:TPU:1, one launch (start us, length us, event | category | flops | bytes accessed | tf_op | source)
XLA Modules:
  0.0 58.3 jit_solution(13586971986875733883)
XLA Ops:
  0.0 0.8 %pad_add_fusion.small_ref = s32[4,128]{1,0:T(4,128)S(1)} fusion(s32[1,8]{1,0:T(1,128)} %bitcast.7, s32[1,3]{1,0:T(1,128)} %param.5, s32[3,128]{1,0:T(4,128)} %param.7), kind=kLoop, calls=%fused_computation | loop fusion | flops 1024 | bytes 3628 | tf_op jit(solution)/shard_map/add | solution.py:318
  0.8 18.7 %shard_map.46 = (f32[8,3,4,128]{3,2,1,0:T(4,128)S(1)}, s32[8,8,128]{2,1,0:T(8,128)S(1)}, s32[1,128]{1,0:T(1,128)S(1)}) custom-call(s32[4,128]{1,0:T(4,128)S(1)} %pad_add_fusion.small_ref, f32[3,64,4,128]{3,2,1,0:T(4,128)} %bitcast.6), custom_call_target="tpu_custom_call" | custom-call | tf_op jit(solution)/shard_map/pallas_call | solution.py:319
  19.5 15.0 %shard_map.47 = f32[9152,128]{1,0:T(8,128)S(1)} custom-call(s32[1,128]{1,0:T(1,128)S(1)} %get-tuple-element.8.counts_ref, f32[8,3,4,128]{3,2,1,0:T(4,128)S(1)} %get-tuple-element.9.x_ref), custom_call_target="tpu_custom_call" | custom-call | tf_op jit(solution)/shard_map/pallas_call | solution.py:189
  34.5 23.1 %shard_map.48 = f32[6,8,128]{2,1,0:T(8,128)S(1)} custom-call(f32[1144,8,128]{2,1,0:T(8,128)S(1)} %bitcast.4, s32[8,8,128]{2,1,0:T(8,128)S(1)} %get-tuple-element.10.word_ref), custom_call_target="tpu_custom_call" | custom-call | tf_op jit(solution)/shard_map/pallas_call | solution.py:472
  57.6 0.6 %copy.6 = f32[8,6,128]{2,0,1:T(8,128)} copy(f32[8,6,128]{2,0,1:T(8,128)S(1)} %bitcast.5) | data formatting | bytes 49152

commit v7 on v6

--- a/solution.py
+++ b/solution.py
@@ -14,7 +14,7 @@
 LINES = 88
 COARSE = 13
 CHUNK = 256
-GROUP = 4
+STRETCHES = (14, 10, 5, 3)
 BATCH = 16
 HOPS = (0, 1, 2, 1)
 ORDER = sorted(
@@ -423,23 +423,18 @@
         def _():
             copy(half).start()
 
-    def second_half(g, _):
-        at = [GROUP * g + u for u in range(GROUP)]
+    def send_next(i, _):
+        send(i)
+        return 0
+
+    start = 0
+    for size in STRETCHES:
+        at = list(range(start, start + size))
         pick_blocks(grid, pick, word_ref, modes, [2 * place(i) + core for i in at], at)
-
-        @pl.when(g == 1)
-        def _():
+        if start == 0:
             pltpu.make_async_copy(handed, handed, recv_sem.at[0]).wait()
-            for u in range(GROUP):
-                send(u)
-
-        @pl.when(g > 0)
-        def _():
-            for i in at:
-                send(i)
-        return 0
-
-    lax.fori_loop(0, chips // GROUP, second_half, 0)
+        lax.fori_loop(start, start + size, send_next, 0)
+        start += size
     parts[slot] = modes[chips - 1]
     most = parts.at[pl.ds(0, 2 * chips - 1)]
     pltpu.make_async_copy(most, most, recv_sem.at[1]).wait()

time: 58.4 us -> 57.9 us (level)
  Pallas kernels: 56.8 us -> 55.9 us
    pallas_call x1, Pallas kernels: 23.1 us -> 22.2 us  [call_factors(): pl.pallas_call(functools.partial(factors_kernel, 1.0 / (FRAMES * total_at...]
where the time goes in v7:
time: 57.9 us; the launch traced here: 57.3 us
  Pallas kernels  55.9 us (97%)
  other arithmetic  0.79 us (1%)
  local copies, waits for them, and re-layouts  0.61 us (1%)
    pallas_call x1, Pallas kernels, call_factors(): pl.pallas_call(functools.partial(factors_kernel, 1.0 / (FRAMES * total_at...  22.2 us
    pallas_call x1, Pallas kernels, call_spread(): pl.pallas_call(spread_kernel, out_shape=(jax.ShapeDtypeStruct((FRAMES, 3,...  18.7 us
    pallas_call x1, Pallas kernels, call_lattice(): pl.pallas_call(lattice_kernel, out_shape=jax.ShapeDtypeStruct((13 * LINES...  15 us

profile of v7, /device:TPU:1, one launch (start us, length us, event | category | flops | bytes accessed | tf_op | source)
XLA Modules:
  0.0 57.3 jit_solution(8059081123717679824)
XLA Ops:
  0.0 0.8 %pad_add_fusion.small_ref = s32[4,128]{1,0:T(4,128)S(1)} fusion(s32[1,8]{1,0:T(1,128)} %bitcast.7, s32[1,3]{1,0:T(1,128)} %param.5, s32[3,128]{1,0:T(4,128)} %param.7), kind=kLoop, calls=%fused_computation | loop fusion | flops 1024 | bytes 3628 | tf_op jit(solution)/shard_map/add | solution.py:318
  0.8 18.7 %shard_map.46 = (f32[8,3,4,128]{3,2,1,0:T(4,128)S(1)}, s32[8,8,128]{2,1,0:T(8,128)S(1)}, s32[1,128]{1,0:T(1,128)S(1)}) custom-call(s32[4,128]{1,0:T(4,128)S(1)} %pad_add_fusion.small_ref, f32[3,64,4,128]{3,2,1,0:T(4,128)} %bitcast.6), custom_call_target="tpu_custom_call" | custom-call | tf_op jit(solution)/shard_map/pallas_call | solution.py:319
  19.5 15.0 %shard_map.47 = f32[9152,128]{1,0:T(8,128)S(1)} custom-call(s32[1,128]{1,0:T(1,128)S(1)} %get-tuple-element.8.counts_ref, f32[8,3,4,128]{3,2,1,0:T(4,128)S(1)} %get-tuple-element.9.x_ref), custom_call_target="tpu_custom_call" | custom-call | tf_op jit(solution)/shard_map/pallas_call | solution.py:189
  34.5 22.2 %shard_map.48 = f32[6,8,128]{2,1,0:T(8,128)S(1)} custom-call(f32[1144,8,128]{2,1,0:T(8,128)S(1)} %bitcast.4, s32[8,8,128]{2,1,0:T(8,128)S(1)} %get-tuple-element.10.word_ref), custom_call_target="tpu_custom_call" | custom-call | tf_op jit(solution)/shard_map/pallas_call | solution.py:467
  56.7 0.6 %copy.6 = f32[8,6,128]{2,0,1:T(8,128)} copy(f32[8,6,128]{2,0,1:T(8,128)S(1)} %bitcast.5) | data formatting | bytes 49152

commit v8 on v7

--- a/solution.py
+++ b/solution.py
@@ -14,7 +14,7 @@
 LINES = 88
 COARSE = 13
 CHUNK = 256
-STRETCHES = (14, 10, 5, 3)
+STRETCHES = (16, 9, 5, 2)
 BATCH = 16
 HOPS = (0, 1, 2, 1)
 ORDER = sorted(

time: 57.9 us -> 58.3 us (level)
  no operation moved by 1% of the time
where the time goes in v8:
time: 58.3 us; the launch traced here: 57.4 us
  Pallas kernels  56 us (96%)
  other arithmetic  0.79 us (1%)
  local copies, waits for them, and re-layouts  0.61 us (1%)
    pallas_call x1, Pallas kernels, call_factors(): pl.pallas_call(functools.partial(factors_kernel, 1.0 / (FRAMES * total_at...  22.3 us
    pallas_call x1, Pallas kernels, call_spread(): pl.pallas_call(spread_kernel, out_shape=(jax.ShapeDtypeStruct((FRAMES, 3,...  18.7 us
    pallas_call x1, Pallas kernels, call_lattice(): pl.pallas_call(lattice_kernel, out_shape=jax.ShapeDtypeStruct((13 * LINES...  15 us

profile of v8, /device:TPU:1, one launch (start us, length us, event | category | flops | bytes accessed | tf_op | source)
XLA Modules:
  0.0 57.4 jit_solution(13161944976329066780)
XLA Ops:
  0.0 0.8 %pad_add_fusion.small_ref = s32[4,128]{1,0:T(4,128)S(1)} fusion(s32[1,8]{1,0:T(1,128)} %bitcast.7, s32[1,3]{1,0:T(1,128)} %param.5, s32[3,128]{1,0:T(4,128)} %param.7), kind=kLoop, calls=%fused_computation | loop fusion | flops 1024 | bytes 3628 | tf_op jit(solution)/shard_map/add | solution.py:318
  0.8 18.7 %shard_map.46 = (f32[8,3,4,128]{3,2,1,0:T(4,128)S(1)}, s32[8,8,128]{2,1,0:T(8,128)S(1)}, s32[1,128]{1,0:T(1,128)S(1)}) custom-call(s32[4,128]{1,0:T(4,128)S(1)} %pad_add_fusion.small_ref, f32[3,64,4,128]{3,2,1,0:T(4,128)} %bitcast.6), custom_call_target="tpu_custom_call" | custom-call | tf_op jit(solution)/shard_map/pallas_call | solution.py:319
  19.5 15.0 %shard_map.47 = f32[9152,128]{1,0:T(8,128)S(1)} custom-call(s32[1,128]{1,0:T(1,128)S(1)} %get-tuple-element.8.counts_ref, f32[8,3,4,128]{3,2,1,0:T(4,128)S(1)} %get-tuple-element.9.x_ref), custom_call_target="tpu_custom_call" | custom-call | tf_op jit(solution)/shard_map/pallas_call | solution.py:189
  34.5 22.3 %shard_map.48 = f32[6,8,128]{2,1,0:T(8,128)S(1)} custom-call(f32[1144,8,128]{2,1,0:T(8,128)S(1)} %bitcast.4, s32[8,8,128]{2,1,0:T(8,128)S(1)} %get-tuple-element.10.word_ref), custom_call_target="tpu_custom_call" | custom-call | tf_op jit(solution)/shard_map/pallas_call | solution.py:467
  56.8 0.6 %copy.6 = f32[8,6,128]{2,0,1:T(8,128)} copy(f32[8,6,128]{2,0,1:T(8,128)S(1)} %bitcast.5) | data formatting | bytes 49152
